TPU v7x, 32 devices: a whole 2x2x4 slice. The times are simulated.
32 devices in a mesh: pix: 8 (over z, y), plane: 4 (over x, core).
Axes of the slice: x: 2, y: 2, z: 4, core: 2. Of those that a mesh axis runs over, the one named last changes fastest.
Arguments:
- movie: bfloat16 [4, 256, 256, 256], P('plane', 'pix'), may hold values from -6 to 6
- footprints: bfloat16 [4, 1024, 1024], P('plane', 'pix'), may hold values from 0 to 0.019897461
- traces: bfloat16 [4, 1024, 256], P('plane', 'pix'), may hold values from 0 to 2
- stripe: int32 [4, 1024, 1], P('plane', 'pix'), may hold values from 0 to 7; in each aligned block of 128 rows (0 to 127, 128 to 255, ..., all dimensions but the last counted through in order) at most 32 rows name the same one
- column: int32 [4, 1024], P('plane', 'pix'), may hold values from 0 to 224
- annulus_gain: float32 [4, 256], P('plane'), may hold values from 1 to 8
- decay_slow: float32 [4, 1024], P('plane', 'pix'), may hold values from 0.4 to 0.9
- decay_fast: float32 [4, 1024], P('plane', 'pix'), may hold values from 0.05 to 0.3
Outputs:
- background: bfloat16 [4, 256, 256, 256], P('plane', 'pix')
- traces_new: float32 [4, 1024, 256], P('plane', 'pix')
Inputs may be any that keep to these rules, and one draw needn't show every extreme that they name: Among the 128 neurons of one device (aligned blocks of 128 neurons of a plane), no stripe is named more than 32 times, and some device names one stripe exactly 32 times.
All inputs are finite; a program needn't handle non-finite values.
Results may differ from a plain program's by a relative error of at most 0.001.
The roundings to bfloat16 on the way count: a program that leaves them out, or rounds other values in their place, can miss the bound.
Values may be sent and summed in bfloat16 or wider, within the bound.
No kernel may reach another device: no remote copies, remote signals or barrier semaphores. Data moves between devices by JAX's collectives and lax.ppermute only.
A program may use at most 128 MiB of HBM per device.

v0:
```python
import functools

import jax
import jax.numpy as jnp
import ml_dtypes
import numpy as np
from jax import lax
from jax.experimental import pallas as pl
from jax.experimental.pallas import tpu as pltpu
from jax.sharding import PartitionSpec as P

FOOT = 32
RAD = 12
GR = 3
LANES = 128
PER = LANES // FOOT
NEAR = PER

lam_floor = 0.1
noise_eps = 1e-05
norm_eps = 1e-05
sigma_twice = 4.5

F32 = jnp.float32
BF16 = jnp.bfloat16
MIB = 1 << 20
ANY = pl.BlockSpec(memory_space=pl.ANY)
VMEM = pl.BlockSpec(memory_space=pltpu.VMEM)


def tap_values():
    offsets = np.arange(-GR, GR + 1).astype(np.float32)
    raw = np.exp(-offsets * offsets / np.float32(sigma_twice)).astype(np.float32)
    return (raw / raw.sum(dtype=np.float32)).astype(ml_dtypes.bfloat16).astype(np.float32)


def params(mib=16):
    return pltpu.CompilerParams(vmem_limit_bytes=mib * MIB)


COST = pl.CostEstimate(flops=1, bytes_accessed=1, transcendentals=0)


def dot(a, b):
    return jnp.dot(a, b, preferred_element_type=F32)


def outbox_kernel(capacity, stripe, column, foot, traces, outbox):
    slots = outbox.shape[0]
    count, tiles = foot.shape
    frames = traces.shape[1]
    before = lax.broadcasted_iota(jnp.int32, (count, count), 0) < lax.broadcasted_iota(
        jnp.int32, (count, count), 1
    )
    named = jnp.broadcast_to(stripe[...].astype(F32), (count, count))
    same = (named == named.T) & before
    rank = jnp.sum(jnp.where(same, 1.0, 0.0), axis=0, keepdims=True).astype(jnp.int32)
    slot = stripe[...] * capacity + rank
    place = lax.broadcasted_iota(jnp.int32, (slots, count), 0)
    left = jnp.broadcast_to(column[...].astype(F32), (LANES, count)).T.astype(BF16)
    lane = lax.broadcasted_iota(jnp.int32, (slots, LANES), 1)
    edge = RAD * FOOT
    lefts = jnp.zeros((slots, LANES), F32)
    at = 3 * frames
    for k, (shift, first, width) in enumerate(
        ((0, 0, tiles), (capacity, 0, edge), (-capacity, tiles - edge, edge))
    ):
        hot = jnp.where(place + shift == slot, 1.0, 0.0).astype(BF16)
        outbox[:, k * frames : (k + 1) * frames] = dot(hot, traces[...]).astype(BF16)
        outbox[:, at : at + width] = dot(hot, foot[:, first : first + width]).astype(BF16)
        lefts = jnp.where(lane == k, dot(hot, left), lefts)
        at += width
    outbox[:, at:] = lefts.astype(BF16)


def make_outbox(stripe, column, foot, traces, capacity, slots):
    count, tiles = foot.shape
    frames = traces.shape[1]
    width = 3 * frames + tiles + 2 * RAD * FOOT + LANES
    return pl.pallas_call(
        functools.partial(outbox_kernel, capacity),
        out_shape=jax.ShapeDtypeStruct((slots, width), BF16),
        compiler_params=params(),
        cost_estimate=COST,
        name="outbox",
    )(stripe, column, foot, traces)


def spread(block, col):
    lane = lax.broadcasted_iota(jnp.int32, block.shape, 1)
    for k in range(7):
        block = jnp.where(((col >> k) & 1) == 1, pltpu.roll(block, 1 << k, 1), block)
    inside = ((lane - col) & (LANES - 1)) < FOOT
    left = inside & (lane >= col)
    right = inside & (lane < col)
    rows = []
    for q in range(PER):
        moved = block if q == 0 else pltpu.roll(block, LANES - q * FOOT, 1)
        rows.append(
            jnp.concatenate(
                [jnp.where(left, moved, 0.0), jnp.where(right, moved, 0.0)], axis=1
            ).astype(BF16)
        )
    return rows


def tile_rows(inbox, which, block, frames):
    lefts = inbox[:, inbox.shape[1] - LANES :].astype(F32)
    col = jnp.broadcast_to(lefts[:, which : which + 1], lefts.shape).astype(jnp.int32)
    start = 3 * frames + block * LANES
    if not isinstance(start, int):
        start = pl.multiple_of(start, LANES)
    return spread(inbox[:, pl.ds(start, LANES)].astype(F32), col)


def model_row(row, inbox, which, frames):
    traces = inbox[:, which * frames : (which + 1) * frames]
    return lax.dot_general(row, traces, (((0,), (0,)), ((), ())), preferred_element_type=F32)


def noise_row(left, change):
    frames = left.shape[1]
    steps = dot(left, change)
    steps = steps * steps
    part = steps[:, 0:LANES]
    for k in range(1, frames // LANES):
        part = part + steps[:, k * LANES : (k + 1) * LANES]
    return jnp.sum(part.T, axis=0, keepdims=True) / (frames - 1)


def change_matrix(frames):
    earlier, later = np.arange(frames)[:, None], np.arange(frames)[None, :]
    steps = (earlier == later + 1).astype(np.float32) - (earlier == later)
    return jnp.asarray(np.where(later < frames - 1, steps, 0.0).astype(ml_dtypes.bfloat16))


def residual_kernel(inbox, movie, change, foot_rows, residual, noise):
    rows, _, frames = movie.shape[1:]

    def group(g, carry):
        noises = []
        for q, row in enumerate(tile_rows(inbox, 0, g, frames)):
            y = g * PER + q
            foot_rows[y] = row
            left = (movie[0, y].astype(F32) - model_row(row, inbox, 0, frames)).astype(BF16)
            residual[y] = left
            noises.append(noise_row(left, change[...]))
        noise[g] = jnp.concatenate(noises, axis=0)
        return carry

    lax.fori_loop(0, rows // PER, group, 0)


def make_residual(inbox, movie, change):
    slots = inbox.shape[0]
    rows, cols, frames = movie.shape[1:]
    foot_rows, residual, noise = pl.pallas_call(
        residual_kernel,
        out_shape=(
            jax.ShapeDtypeStruct((rows, slots, cols), BF16),
            jax.ShapeDtypeStruct((rows, cols, frames), BF16),
            jax.ShapeDtypeStruct((rows // PER, PER, cols), F32),
        ),
        compiler_params=params(),
        cost_estimate=COST,
        name="residual",
    )(inbox, movie, change)
    return foot_rows, residual, noise.reshape(rows, cols)


def near_kernel(inbox, movie_next, movie_prev, change, foot_rows, residual, noise):
    frames = movie_next.shape[2]
    own = FOOT // PER
    for side, (block, movie) in enumerate(
        ((own, movie_next), (own + 2 * RAD // PER - 1, movie_prev))
    ):
        for q, row in enumerate(tile_rows(inbox, 1 + side, block, frames)):
            y = side * NEAR + q
            foot_rows[y] = row
            left = movie[q].astype(F32) - model_row(row, inbox, 1 + side, frames)
            left = left.astype(BF16)
            residual[y] = left
            noise[y : y + 1, :] = noise_row(left, change[...])


def make_near(inbox, movie_next, movie_prev, change):
    slots = inbox.shape[0]
    cols, frames = movie_next.shape[1:]
    return pl.pallas_call(
        near_kernel,
        out_shape=(
            jax.ShapeDtypeStruct((2 * NEAR, slots, cols), BF16),
            jax.ShapeDtypeStruct((2 * NEAR, cols, frames), BF16),
            jax.ShapeDtypeStruct((2 * NEAR, cols), F32),
        ),
        compiler_params=params(),
        cost_estimate=COST,
        name="near",
    )(inbox, movie_next, movie_prev, change)


def outer_kernel(inbox, *models):
    frames = models[0].shape[2]
    own = FOOT // PER
    groups = RAD // PER
    for piece, model in enumerate(models, 1):
        for side, block in enumerate((own + piece, own + 2 * groups - 1 - piece)):
            for q, row in enumerate(tile_rows(inbox, 1 + side, block, frames)):
                model[side * PER + q] = model_row(row, inbox, 1 + side, frames)


def make_outer_models(inbox, cols, frames):
    piece = jax.ShapeDtypeStruct((2 * PER, cols, frames), F32)
    return pl.pallas_call(
        outer_kernel,
        out_shape=(piece,) * (RAD // PER - 1),
        compiler_params=params(),
        cost_estimate=COST,
        name="outer_models",
    )(inbox)


def weights_kernel(taps, part, own, near, scale, band, out, out_next, out_prev):
    rows, slots, cols = own.shape

    def across(foot, inv):
        scaled = (foot.astype(F32) * inv[:, None, :]).astype(BF16)
        count = foot.shape[0]
        return dot(scaled.reshape(count * part, cols), band[...]).reshape(count, part, cols)

    def some(i, carry):
        these = pl.ds(pl.multiple_of(i * part, part), part)
        blurred = across(own[:, these, :], scale[NEAR : NEAR + rows])
        for r in range(rows):
            total = taps[GR] * blurred[r]
            for k in range(1, GR + 1):
                if r - k >= 0 and r + k < rows:
                    total = total + taps[GR + k] * (blurred[r - k] + blurred[r + k])
                elif r - k >= 0:
                    total = total + taps[GR + k] * blurred[r - k]
                elif r + k < rows:
                    total = total + taps[GR + k] * blurred[r + k]
            out[r, these, :] = total.astype(BF16)
        after = across(near[0:GR, these, :], scale[0:GR])
        ahead = across(near[2 * NEAR - GR : 2 * NEAR, these, :], scale[rows + 2 * NEAR - GR :])
        for a in range(GR):
            total = taps[2 * GR - a] * after[0]
            for r in range(1, a + 1):
                total = total + taps[2 * GR + r - a] * after[r]
            out_next[a, these, :] = total.astype(BF16)
            total = taps[2 * GR] * ahead[a]
            for b in range(a + 1, GR):
                total = total + taps[2 * GR + a - b] * ahead[b]
            out_prev[a, these, :] = total.astype(BF16)
        return carry

    lax.fori_loop(0, slots // part, some, 0)


def make_weights(foot_rows, near_rows, scale):
    rows, slots, cols = foot_rows.shape
    taps = tap_values()
    lag = np.arange(cols)[:, None] - np.arange(cols)[None, :]
    band = np.where(np.abs(lag) <= GR, taps[np.clip(lag + GR, 0, 2 * GR)], 0.0)
    band = jnp.asarray(band.astype(ml_dtypes.bfloat16))
    return pl.pallas_call(
        functools.partial(weights_kernel, [float(t) for t in taps], 32),
        out_shape=(
            jax.ShapeDtypeStruct((rows, slots, cols), BF16),
            jax.ShapeDtypeStruct((GR, slots, cols), BF16),
            jax.ShapeDtypeStruct((GR, slots, cols), BF16),
        ),
        compiler_params=params(),
        cost_estimate=COST,
        name="weights",
    )(foot_rows, near_rows, scale, band)


def annulus_group(g, own, leaving, entering, weight, gain, band, column, total, outgoing):
    cols, frames = own.shape[1:]
    top = lax.broadcasted_iota(jnp.int32, (cols // 8, 8, LANES), 1) < 4
    blank = jnp.zeros((2, 8, LANES), F32)
    outs = [leaving(q) for q in range(PER)]
    news = [entering(q) for q in range(PER)]
    levels = [dot(band, jnp.concatenate([o, n], axis=0)) for o, n in zip(outs, news)]
    column = list(column)
    dets = []
    for q in range(PER):
        det = []
        for h in range(frames // LANES):
            part = slice(h * LANES, (h + 1) * LANES)
            inner = column[h] - outs[q][:, part].astype(F32)
            column[h] = inner + news[q][:, part].astype(F32)
            turned = pltpu.roll(inner.reshape(cols // 8, 8, LANES), 4, 1)
            turned = jnp.concatenate([blank, turned, blank], axis=0)
            both = turned[0 : cols // 8 + 1] + turned[3 : cols // 8 + 4]
            sides = jnp.where(top, both[0 : cols // 8], both[1 : cols // 8 + 1])
            fit = (levels[q][:, part] + sides.reshape(cols, LANES)) * gain
            outgoing[g, q, :, part] = fit.astype(BF16)
            det.append((own[g * PER + q, :, part].astype(F32) - fit).astype(BF16))
        dets.append(jnp.concatenate(det, axis=1))
    weights = jnp.concatenate([weight[g * PER + q] for q in range(PER)], axis=1)
    total = total + dot(weights, jnp.concatenate(dets, axis=0))
    return column, total, dets


def halves(ref):
    return [ref[:, h * LANES : (h + 1) * LANES] for h in range(ref.shape[1] // LANES)]


def add_rows(column, rows, sign=1.0):
    for row in rows:
        column = [c + sign * r.astype(F32) for c, r in zip(column, halves(row))]
    return column


def put(ref, column):
    for h, value in enumerate(column):
        ref[:, h * LANES : (h + 1) * LANES] = value


def subtracted(movie, model, first):
    return [(movie[r].astype(F32) - model[first + r]).astype(BF16) for r in range(PER)]


def sender(outgoing, background, sems):
    def send(g, slot):
        return pltpu.make_async_copy(
            outgoing.at[g], background.at[0, pl.ds(g * PER, PER)], sems.at[slot]
        )

    return send


def middle_kernel(
    own, near, weight, gain, band, background, upper, lower, total, outgoing, sems
):
    rows, cols, frames = own.shape
    first, last = RAD // PER - 1, (rows - RAD) // PER + 1
    send = sender(outgoing, background, sems)
    column = add_rows([jnp.zeros((cols, LANES), F32)] * (frames // LANES), [
        near[NEAR + r] for r in range(NEAR)
    ])
    column = add_rows(column, [own[r] for r in range(RAD + NEAR)])
    put(upper, column)
    column = add_rows(column, [own[RAD + NEAR + r] for r in range(PER)])
    grown = jnp.zeros(total.shape, F32)
    for k, g in enumerate(range(first, last)):
        y = g * PER
        column, grown, _ = annulus_group(
            g,
            own,
            (lambda q: near[NEAR + q]) if g == first else (lambda q: own[y - RAD + q]),
            (lambda q: near[q]) if g == last - 1 else (lambda q: own[y + RAD + q]),
            weight, gain[...], band[...], column, grown, outgoing,
        )
        send(g, k).start()
    put(lower, column)
    total[...] = grown
    for k, g in enumerate(range(first, last)):
        send(g, k).wait()


def mid_kernel(
    own, near, movie_prev, movie_next, model, weight, gain, band, before, upper, lower, total,
    background, new_upper, new_lower, new_total, outgoing, sems,
):
    del before
    rows = own.shape[0]
    low, high = RAD // PER - 2, (rows - RAD) // PER + 1
    send = sender(outgoing, background, sems)
    above, below = subtracted(movie_prev, model, PER), subtracted(movie_next, model, 0)
    column = add_rows(halves(upper), above)
    put(new_upper, add_rows(column, [own[RAD + r] for r in range(PER)], -1.0))
    y = low * PER
    _, grown, _ = annulus_group(
        low, own, lambda q: above[q], lambda q: own[y + RAD + q],
        weight, gain[...], band[...], column, total[...], outgoing,
    )
    send(low, 0).start()
    z = high * PER
    column, grown, _ = annulus_group(
        high, own, lambda q: own[z - RAD + q], lambda q: below[q],
        weight, gain[...], band[...], halves(lower), grown, outgoing,
    )
    send(high, 1).start()
    put(new_lower, column)
    new_total[...] = grown
    send(low, 0).wait()
    send(high, 1).wait()


def end_kernel(
    own, movie_prev, movie_next, model, weight, weight_next, weight_prev, gain, band, before,
    upper, lower, total, background, gradient, outgoing, sems,
):
    del before
    rows, _, frames = own.shape
    low, high = 0, rows // PER - 1
    send = sender(outgoing, background, sems)
    above, below = subtracted(movie_prev, model, PER), subtracted(movie_next, model, 0)
    _, grown, low_dets = annulus_group(
        low, own, lambda q: above[q], lambda q: own[RAD + q],
        weight, gain[...], band[...], add_rows(halves(upper), above), total[...], outgoing,
    )
    send(low, 0).start()
    z = high * PER
    _, grown, high_dets = annulus_group(
        high, own, lambda q: own[z - RAD + q], lambda q: below[q],
        weight, gain[...], band[...], halves(lower), grown, outgoing,
    )
    send(high, 1).start()
    for at, edge, dets in ((2, weight_next, high_dets[PER - GR :]), (3, weight_prev, low_dets[:GR])):
        value = dot(
            jnp.concatenate([edge[a] for a in range(GR)], axis=1), jnp.concatenate(dets, axis=0)
        )
        gradient[:, at * frames : (at + 1) * frames] = value.astype(BF16)
    upper_half = grown.astype(BF16)
    gradient[:, 0:frames] = upper_half
    gradient[:, frames : 2 * frames] = (grown - upper_half.astype(F32)).astype(BF16)
    send(low, 0).wait()
    send(high, 1).wait()


def make_annulus(own, near, movies, models, weights, gain):
    rows, cols, frames = own.shape
    weight, weight_next, weight_prev = weights
    slots = weight.shape[1]
    lag = np.arange(cols)[:, None] - np.arange(cols)[None, :]
    band = (np.abs(lag) <= RAD).astype(ml_dtypes.bfloat16)
    band = jnp.asarray(np.concatenate([band, band], axis=1))
    background = jax.ShapeDtypeStruct((1, rows, cols, frames), BF16)
    column = jax.ShapeDtypeStruct((cols, frames), F32)
    total = jax.ShapeDtypeStruct((slots, frames), F32)
    gradient = jax.ShapeDtypeStruct((slots, 4 * frames), BF16)

    def call(kernel, name, args, outs, done):
        specs = [VMEM] * len(args)
        if done is not None:
            specs[done] = ANY
        return pl.pallas_call(
            kernel,
            in_specs=specs,
            out_specs=[ANY] + [VMEM] * (len(outs) - 1),
            out_shape=outs,
            scratch_shapes=[
                pltpu.VMEM((rows // PER, PER, cols, frames), BF16),
                pltpu.SemaphoreType.DMA((rows // PER,)),
            ],
            input_output_aliases={} if done is None else {done: 0},
            compiler_params=params(),
            cost_estimate=COST,
            name=name,
        )(*args)

    done, upper, lower, grown = call(
        middle_kernel, "annulus_middle", (own, near, weight, gain, band),
        (background, column, column, total), None,
    )
    done, upper, lower, grown = call(
        mid_kernel, "annulus_mid",
        (own, near, *movies[0], models[0], weight, gain, band, done, upper, lower, grown),
        (background, column, column, total), 8,
    )
    return call(
        end_kernel, "annulus_end",
        (own, *movies[1], models[1], weight, weight_next, weight_prev, gain, band, done, upper,
         lower, grown),
        (background, gradient), 9,
    )


def traces_kernel(capacity, stripe, slow, fast, step, traces, inbox, out):
    count, frames = traces.shape
    slots = inbox.shape[0]

    def upended(row):
        return jnp.broadcast_to(row[...].astype(F32), (LANES, count)).T

    before = lax.broadcasted_iota(jnp.int32, (count, count), 1) < lax.broadcasted_iota(
        jnp.int32, (count, count), 0
    )
    named = upended(stripe)
    same = (named == stripe[...].astype(F32)) & before
    rank = jnp.sum(jnp.where(same, 1.0, 0.0), axis=1, keepdims=True)
    slot = (named[:, 0:1] * capacity + rank).astype(jnp.int32)
    place = lax.broadcasted_iota(jnp.int32, (count, slots), 1)

    def onehot(shift):
        return jnp.where(place + shift == slot, 1.0, 0.0).astype(BF16)

    here = onehot(0)
    gradient = (
        dot(here, inbox[:, 0:frames])
        + dot(here, inbox[:, frames : 2 * frames])
        + dot(onehot(capacity), inbox[:, 2 * frames : 3 * frames])
        + dot(onehot(-capacity), inbox[:, 3 * frames : 4 * frames])
    )

    def wide(row):
        return jnp.concatenate([upended(row)] * (frames // LANES), axis=1)

    updated = traces[...].astype(F32) + wide(step) * gradient
    lane = lax.broadcasted_iota(jnp.int32, (count, frames), 1)

    def lagged(value, lag):
        return jnp.where(lane >= lag, pltpu.roll(value, lag, 1), 0.0)

    a, b = wide(slow), wide(fast)
    driven = updated - (a + b) * lagged(updated, 1) + (a * b) * lagged(updated, 2)
    value = jnp.maximum(driven - lam_floor, 0.0) * ((1.0 - a) * (1.0 - b))
    for root in (a, b):
        lag = 1
        while lag < frames:
            value = value + root * lagged(value, lag)
            root = root * root
            lag *= 2
    out[...] = value


def make_traces(stripe, slow, fast, step, traces, inbox, capacity):
    count, frames = traces.shape
    return pl.pallas_call(
        functools.partial(traces_kernel, capacity),
        out_shape=jax.ShapeDtypeStruct((count, frames), F32),
        compiler_params=params(),
        cost_estimate=COST,
        name="traces",
    )(stripe, slow, fast, step, traces, inbox)


def neighbours(axis):
    devices = lax.axis_size(axis)
    up = [(i, i + 1) for i in range(devices - 1)]
    return up, [(j, i) for i, j in up]


def on_device(movie, footprints, traces, stripe, column, annulus_gain, decay_slow, decay_fast):
    pix_count = lax.axis_size("pix")
    rows, cols, frames = movie.shape[1:]
    count = footprints.shape[1]
    capacity = max(2, 2 * count // pix_count)
    slots = pix_count * capacity
    pix_up, pix_down = neighbours("pix")
    plane_up, plane_down = neighbours("plane")

    stripe_row = stripe.reshape(1, count)
    outbox = make_outbox(stripe_row, column, footprints[0], traces[0], capacity, slots)
    cuts = [
        (movie[0, rows - (k + 1) * PER : rows - k * PER], movie[0, k * PER : (k + 1) * PER])
        for k in range(RAD // PER)
    ]

    cuts[1:], outbox = lax.optimization_barrier((cuts[1:], outbox))
    inbox = lax.all_to_all(outbox, "pix", split_axis=0, concat_axis=0, tiled=True)

    def exchange(cut):
        return (lax.ppermute(cut[0], "pix", pix_up), lax.ppermute(cut[1], "pix", pix_down))

    near_prev, near_next = exchange(cuts[0])
    mid, far = exchange(cuts[1]), exchange(cuts[2])

    change = change_matrix(frames)
    foot_rows, residual, noise = make_residual(inbox, movie, change)
    near_rows, near_residual, near_noise = make_near(inbox, near_next, near_prev, change)
    noise = jnp.concatenate([near_noise[:NEAR], noise, near_noise[NEAR:]], axis=0)
    noise_before = lax.ppermute(noise, "plane", plane_up)
    noise_after = lax.ppermute(noise, "plane", plane_down)
    pooled = (noise_before + 2.0 * noise + noise_after) / 4.0
    scale = 1.0 / jnp.sqrt(pooled + noise_eps)

    weights = make_weights(foot_rows, near_rows, scale)
    models = make_outer_models(inbox, cols, frames)

    gain = jnp.broadcast_to((annulus_gain[0] / (8.0 * RAD))[:, None], (cols, LANES))
    background, gradient = make_annulus(
        residual, near_residual, (mid, far), models, weights, gain
    )
    home = lax.all_to_all(gradient, "pix", split_axis=0, concat_axis=0, tiled=True)
    foot_f = footprints[0].astype(F32)
    step = 1.0 / (jnp.sum(foot_f * foot_f, axis=1) + norm_eps)
    traces_new = make_traces(
        stripe_row, decay_slow, decay_fast, step[None], traces[0], home, capacity
    )
    return (background, traces_new[None])


def solution(mesh):
    placed = (
        P("plane", "pix", None, None),
        P("plane", "pix", None),
        P("plane", "pix", None),
        P("plane", "pix", None),
        P("plane", "pix"),
        P("plane", None),
        P("plane", "pix"),
        P("plane", "pix"),
    )
    return jax.shard_map(
        on_device,
        mesh=mesh,
        in_specs=placed,
        out_specs=(P("plane", "pix", None, None), P("plane", "pix", None)),
        check_vma=False,
    )
```

profile of v0, /device:TPU:0, one launch (start us, length us, event | category | flops | bytes accessed | tf_op | source)
XLA Modules:
  0.0 144.5 jit_solution(17990865350590006554)
XLA Ops:
  0.6 0.0 copy-start.13
  0.6 0.0 copy-start.18
  0.7 0.0 copy-start.19
  0.7 0.0 copy-start.6
  0.7 0.0 copy-start.15
  0.7 3.6 %slice_bitcast_fusion = (bf16[4,256,256]{2,1,0:T(8,128)(2,1)}, bf16[4,256,256]{2,1,0:T(8,128)(2,1)}, bf16[4,256,256]{2,1,0:T(8,128)(2,1)}, bf16[4,256,256]{2,1,0...) fusion(bf16[1,32,256,256]{3,2,1,0:T(8,128)(2,1)} %movie.1), kind=kLoop, calls=%fused_computation.1 | loop fusion | bytes 6291456 | tf_op jit(solution)/shard_map/squeeze | solution.py:550
  4.3 0.0 copy-done.18
  4.3 0.0 copy-done.19
  4.3 0.0 copy-done.6
  4.3 0.0 copy-done.15
  4.3 1.7 %outbox.1 = bf16[256,2688]{1,0:T(8,128)(2,1)} custom-call(s32[1,128]{1,0:T(1,128)S(1)} %bitcast.31, s32[1,128]{1,0:T(1,128)S(1)} %copy-done.19, bf16[128,1024]{1,0:T(8,128)(2,1)S(1)} %bitcast.28, bf16[128,256]{1,0:T(8,128)(2,1)S(1)} %bitcast.29), custom_call_target="tpu_custom_call" | custom-call | flops 1 | bytes 1 | tf_op jit(solution)/shard_map/outbox/pallas_call | solution.py:80
  6.1 7.3 %all-to-all-start = ((bf16[8,32,2688]{2,1,0:T(8,128)(2,1)}), bf16[8,32,2688]{2,1,0:T(8,128)(2,1)S(1)}, u32[]{:S(2)}, u32[]{:S(2)}) async-start(bf16[8,32,2688]{2,1,0:T(8,128)(2,1)} %bitcast.7), calls=%async_computation | async-start | bytes 2752512 | tf_op jit(solution)/shard_map/all_to_all | solution.py:555
  13.4 1.3 collective-permute-start.2
  14.6 4.6 %collective-permute-start.3 = (bf16[4,256,256]{2,1,0:T(8,128)(2,1)}, bf16[4,256,256]{2,1,0:T(8,128)(2,1)S(1)}, u32[]{:S(2)}, u32[]{:S(2)}) collective-permute-start(bf16[4,256,256]{2,1,0:T(8,128)(2,1)} %get-tuple-element.54), channel_id=1, source_target_pairs={{0,4},{4,8},{8,12},{12,16},{16,20},{20,24},{24,28},{1,5},{5,9},{9,... | collective-permute-start | bytes 1572872 | tf_op jit(solution)/shard_map/ppermute | solution.py:558
  19.2 4.8 %collective-permute-start = (bf16[4,256,256]{2,1,0:T(8,128)(2,1)}, bf16[4,256,256]{2,1,0:T(8,128)(2,1)S(1)}, u32[]{:S(2)}, u32[]{:S(2)}) collective-permute-start(bf16[4,256,256]{2,1,0:T(8,128)(2,1)} %get-tuple-element.30), channel_id=1, source_target_pairs={{0,4},{4,8},{8,12},{12,16},{16,20},{20,24},{24,28},{1,5},{5,9},{9,... | collective-permute-start | bytes 1572872 | tf_op jit(solution)/shard_map/ppermute | solution.py:558
  24.1 1.3 collective-permute-start.1
  25.4 5.4 %collective-permute-start.6 = (bf16[4,256,256]{2,1,0:T(8,128)(2,1)}, bf16[4,256,256]{2,1,0:T(8,128)(2,1)}, u32[]{:S(2)}, u32[]{:S(2)}) collective-permute-start(bf16[4,256,256]{2,1,0:T(8,128)(2,1)} %get-tuple-element.41), channel_id=1, source_target_pairs={{0,4},{4,8},{8,12},{12,16},{16,20},{20,24},{24,28},{1,5},{5,9},{9,... | collective-permute-start | bytes 1572872 | tf_op jit(solution)/shard_map/ppermute | solution.py:558
  30.8 16.8 %all-to-all-done = bf16[8,32,2688]{2,1,0:T(8,128)(2,1)S(1)} async-done(((bf16[8,32,2688]{2,1,0:T(8,128)(2,1)}), bf16[8,32,2688]{2,1,0:T(8,128)(2,1)S(1)}, u32[]{:S(2)}, u32[]{:S(2)}) %all-to-all-start) | async-done | bytes 1376288 | tf_op jit(solution)/shard_map/all_to_all | solution.py:555
  47.6 0.0 copy-done.13
  47.6 2.2 %copy-done.2 = bf16[1,32,256,256]{3,2,1,0:T(8,128)(2,1)S(1)} copy-done((bf16[1,32,256,256]{3,2,1,0:T(8,128)(2,1)S(1)}, bf16[1,32,256,256]{3,2,1,0:T(8,128)(2,1)}, u32[]{:S(2)}) %copy-start.2) | copy-done | bytes 4194328
  49.8 10.1 %residual.1 = (bf16[32,256,256]{2,1,0:T(8,128)(2,1)S(1)}, bf16[32,256,256]{2,1,0:T(8,128)(2,1)S(1)}, f32[8,4,256]{2,1,0:T(4,128)S(1)}) custom-call(bf16[256,2688]{1,0:T(8,128)(2,1)S(1)} %bitcast.24, bf16[1,32,256,256]{3,2,1,0:T(8,128)(2,1)S(1)} %copy-done.2, bf16[256,256]{1,0:T(8,128)(2,1)S(1)} %copy-done.13), custom_call_target="tpu_custom_call" | custom-call | flops 1 | bytes 1 | tf_op jit(solution)/shard_map/residual/pallas_call | solution.py:157
  59.9 0.0 copy-start
  59.9 2.0 %copy-done = bf16[32,256,256]{2,1,0:T(8,128)(2,1)} copy-done((bf16[32,256,256]{2,1,0:T(8,128)(2,1)}, bf16[32,256,256]{2,1,0:T(8,128)(2,1)S(1)}, u32[]{:S(2)}) %copy-start) | copy-done | bytes 4194328
  61.9 2.0 %copy-done.3 = bf16[32,256,256]{2,1,0:T(8,128)(2,1)} copy-done((bf16[32,256,256]{2,1,0:T(8,128)(2,1)}, bf16[32,256,256]{2,1,0:T(8,128)(2,1)S(1)}, u32[]{:S(2)}) %copy-start.3) | copy-done | bytes 4194328
  63.9 0.6 copy-done.17
  64.5 0.0 collective-permute-done.2.movie_next
  64.5 0.8 copy-done.9
  65.3 1.3 collective-permute-start.7
  66.6 0.0 collective-permute-done.3.movie_prev
  66.6 0.0 copy-start.11
  66.6 0.8 copy-done.11
  67.4 1.0 copy-done.10
  68.5 1.0 copy-done.12
  69.5 0.9 copy-done.14
  70.4 1.9 %near.1 = (bf16[8,256,256]{2,1,0:T(8,128)(2,1)S(1)}, bf16[8,256,256]{2,1,0:T(8,128)(2,1)S(1)}, f32[8,256]{1,0:T(8,128)S(1)}) custom-call(bf16[256,2688]{1,0:T(8,128)(2,1)S(1)} %bitcast.25, bf16[4,256,256]{2,1,0:T(8,128)(2,1)S(1)} %copy-done.10, bf16[4,256,256]{2,1,0:T(8,128)(2,1)S(1)} %copy-done.12, bf16[256,256]{1,0:T(8,128)(2,1)S(1)} %copy-done.14), custom_call_target="tpu_custom_call" | custom-call | flops 1 | bytes 1 | tf_op jit(solution)/shard_map/near/pallas_call | solution.py:189
  72.4 1.0 copy-done.7
  73.4 1.4 reshape.36
  74.8 0.9 pad_maximum_fusion
  75.7 1.4 collective-permute-start.5
  77.1 1.8 %collective-permute-done.5 = f32[40,256]{1,0:T(8,128)S(1)} collective-permute-done((f32[40,256]{1,0:T(8,128)S(1)}, f32[40,256]{1,0:T(8,128)S(1)}, u32[]{:S(2)}, u32[]{:S(2)}) %collective-permute-start.5) | collective-permute-done | bytes 40992 | tf_op jit(solution)/shard_map/ppermute | solution.py:568
  78.9 4.2 %collective-permute-start.4 = (f32[40,256]{1,0:T(8,128)S(1)}, f32[40,256]{1,0:T(8,128)S(1)}, u32[]{:S(2)}, u32[]{:S(2)}) collective-permute-start(f32[40,256]{1,0:T(8,128)S(1)} %pad_maximum_fusion), channel_id=1, source_target_pairs={{0,1},{1,2},{2,3},{4,5},{5,6},{6,7},{8,9},{9,10},{10,11},{12,13},{... | collective-permute-start | bytes 122888 | tf_op jit(solution)/shard_map/ppermute | solution.py:567
  83.1 0.0 copy-done.22
  83.1 2.8 %outer_models.1 = (f32[8,256,256]{2,1,0:T(8,128)S(1)}, f32[8,256,256]{2,1,0:T(8,128)S(1)}) custom-call(bf16[256,2688]{1,0:T(8,128)(2,1)S(1)} %bitcast.26), custom_call_target="tpu_custom_call" | custom-call | flops 1 | bytes 1 | tf_op jit(solution)/shard_map/outer_models/pallas_call | solution.py:214
  85.9 0.0 collective-permute-done.4
  85.9 0.8 add_rsqrt_fusion.scale
  86.7 0.0 copy-start.4
  86.7 2.2 %copy-done.4 = bf16[32,256,256]{2,1,0:T(8,128)(2,1)S(1)} copy-done((bf16[32,256,256]{2,1,0:T(8,128)(2,1)S(1)}, bf16[32,256,256]{2,1,0:T(8,128)(2,1)}, u32[]{:S(2)}) %copy-start.4) | copy-done | bytes 4194328
  88.8 1.2 copy-done.8
  90.1 0.9 copy-done.16
  91.0 4.7 %weights.1 = (bf16[32,256,256]{2,1,0:T(8,128)(2,1)S(1)}, bf16[3,256,256]{2,1,0:T(8,128)(2,1)S(1)}, bf16[3,256,256]{2,1,0:T(8,128)(2,1)S(1)}) custom-call(bf16[32,256,256]{2,1,0:T(8,128)(2,1)S(1)} %copy-done.4, bf16[8,256,256]{2,1,0:T(8,128)(2,1)S(1)} %copy-done.8, f32[40,256]{1,0:T(8,128)S(1)} %add_rsqrt_fusion.scale, bf16[256,256]{1,0:T(8,128)(2,1)S(1)} %copy-done.16), custom_call_target="tpu_custom_call" | custom-call | flops 1 | bytes 1 | tf_op jit(solution)/shard_map/weights/pallas_call | solution.py:266
  95.7 0.1 broadcast_in_dim.4.gain
  95.8 4.0 %annulus_middle.1 = (bf16[1,32,256,256]{3,2,1,0:T(8,128)(2,1)}, f32[256,256]{1,0:T(8,128)S(1)}, f32[256,256]{1,0:T(8,128)S(1)}, f32[256,256]{1,0:T(8,128)S(1)}) custom-call(bf16[32,256,256]{2,1,0:T(8,128)(2,1)S(1)} %copy-done.1, bf16[8,256,256]{2,1,0:T(8,128)(2,1)S(1)} %get-tuple-element.40.near, bf16[32,256,256]{2,1,0:T(8,128)(2,1)S(1)} %get-tuple-element.37.weight, ...), custom_call_target="tpu_custom_call" | custom-call | flops 1 | bytes 1 | tf_op jit(solution)/shard_map/annulus_middle/pallas_call | solution.py:441
  99.8 0.0 collective-permute-done.6.movie_prev
  99.8 0.0 collective-permute-done.7.movie_next
  99.8 3.6 %annulus_mid.1 = (bf16[1,32,256,256]{3,2,1,0:T(8,128)(2,1)}, f32[256,256]{1,0:T(8,128)S(1)}, f32[256,256]{1,0:T(8,128)S(1)}, f32[256,256]{1,0:T(8,128)S(1)}) custom-call(bf16[32,256,256]{2,1,0:T(8,128)(2,1)S(1)} %copy-done.1, bf16[8,256,256]{2,1,0:T(8,128)(2,1)S(1)} %get-tuple-element.40.near, ...), custom_call_target="tpu_custom_call", output_to_operand_aliasing={{0}: (8, {})} | custom-call | flops 1 | bytes 1 | tf_op jit(solution)/shard_map/annulus_mid/pallas_call | solution.py:441
  103.4 0.0 collective-permute-done.movie_prev
  103.5 0.0 collective-permute-done.1.movie_next
  103.5 0.0 copy-start.20
  103.5 0.0 copy-start.21
  103.5 4.4 %annulus_end.1 = (bf16[1,32,256,256]{3,2,1,0:T(8,128)(2,1)}, bf16[256,1024]{1,0:T(8,128)(2,1)}) custom-call(bf16[32,256,256]{2,1,0:T(8,128)(2,1)S(1)} %copy-done.1, bf16[4,256,256]{2,1,0:T(8,128)(2,1)S(1)} %collective-permute-done.movie_prev, bf16[4,256,256]{2,1,0:T(8,128)(2,1)} %collective-permute-done.1.movie_next, ...), custom_call_target="tpu_custom_call", output_to_operand_aliasing={{0}: (9, {})} | custom-call | flops 1 | bytes 1 | tf_op jit(solution)/shard_map/annulus_end/pallas_call | solution.py:441
  107.9 19.7 %all-to-all-start.1 = ((bf16[8,32,1024]{2,1,0:T(8,128)(2,1)}), bf16[8,32,1024]{2,1,0:T(8,128)(2,1)S(1)}, u32[]{:S(2)}, u32[]{:S(2)}) async-start(bf16[8,32,1024]{2,1,0:T(8,128)(2,1)} %bitcast.13), calls=%async_computation.1 | async-start | bytes 1048576 | tf_op jit(solution)/shard_map/all_to_all | solution.py:579
  127.6 0.1 multiply_reduce_fusion
  127.7 14.5 %all-to-all-done.1 = bf16[8,32,1024]{2,1,0:T(8,128)(2,1)S(1)} async-done(((bf16[8,32,1024]{2,1,0:T(8,128)(2,1)}), bf16[8,32,1024]{2,1,0:T(8,128)(2,1)S(1)}, u32[]{:S(2)}, u32[]{:S(2)}) %all-to-all-start.1) | async-done | bytes 524320 | tf_op jit(solution)/shard_map/all_to_all | solution.py:579
  142.3 2.2 %traces.1 = f32[128,256]{1,0:T(8,128)} custom-call(s32[1,128]{1,0:T(1,128)S(1)} %bitcast.32, f32[1,128]{1,0:T(1,128)S(1)} %copy-done.20, f32[1,128]{1,0:T(1,128)S(1)} %copy-done.21, f32[1,128]{1,0:T(1,128)S(1)} %divide_bitcast_fusion.step, bf16[128,256]{1,0:T(8,128)(2,1)S(1)} %bitcast.30, bf16[256,1024]{1,0:T(8,128)(2,1)S(1)} %bitcast.27), custom_call_target="tpu_custom_call" | custom-call | flops 1 | bytes 1 | tf_op jit(solution)/shard_map/traces/pallas_call | solution.py:523
  (20 shorter events, 0.0 us)
Async XLA Ops:
  0.6 47.0 %copy-start.13 = (bf16[256,256]{1,0:T(8,128)(2,1)S(1)}, bf16[256,256]{1,0:T(8,128)(2,1)}, u32[]{:S(2)}) copy-start(bf16[256,256]{1,0:T(8,128)(2,1)} %constant.22.clone.change) | copy-start | bytes 393220
  0.6 3.7 %copy-start.18 = (s32[1,128,1]{1,2,0:T(1,128)S(1)}, s32[1,128,1]{1,2,0:T(1,128)}, u32[]{:S(2)}) copy-start(s32[1,128,1]{1,2,0:T(1,128)} %param.14) | copy-start | bytes 1540
  0.7 3.7 %copy-start.19 = (s32[1,128]{1,0:T(1,128)S(1)}, s32[1,128]{1,0:T(1,128)}, u32[]{:S(2)}) copy-start(s32[1,128]{1,0:T(1,128)} %column.1) | copy-start | bytes 1540
  0.7 3.7 %copy-start.6 = (bf16[1,128,1024]{2,1,0:T(8,128)(2,1)S(1)}, bf16[1,128,1024]{2,1,0:T(8,128)(2,1)}, u32[]{:S(2)}) copy-start(bf16[1,128,1024]{2,1,0:T(8,128)(2,1)} %param.12) | copy-start | bytes 786436
  0.7 3.7 %copy-start.15 = (bf16[1,128,256]{2,1,0:T(8,128)(2,1)S(1)}, bf16[1,128,256]{2,1,0:T(8,128)(2,1)}, u32[]{:S(2)}) copy-start(bf16[1,128,256]{2,1,0:T(8,128)(2,1)} %param.13) | copy-start | bytes 196612
  6.1 41.5 %all-to-all-start = ((bf16[8,32,2688]{2,1,0:T(8,128)(2,1)}), bf16[8,32,2688]{2,1,0:T(8,128)(2,1)S(1)}, u32[]{:S(2)}, u32[]{:S(2)}) async-start(bf16[8,32,2688]{2,1,0:T(8,128)(2,1)} %bitcast.7), calls=%async_computation | async-start | bytes 2752512 | tf_op jit(solution)/shard_map/all_to_all | solution.py:555
  13.4 51.2 %collective-permute-start.2 = (bf16[4,256,256]{2,1,0:T(8,128)(2,1)}, bf16[4,256,256]{2,1,0:T(8,128)(2,1)S(1)}, u32[]{:S(2)}, u32[]{:S(2)}) collective-permute-start(bf16[4,256,256]{2,1,0:T(8,128)(2,1)} %get-tuple-element.59), channel_id=1, source_target_pairs={{4,0},{8,4},{12,8},{16,12},{20,16},{24,20},{28,24},{5,1},{9,5},{13... | collective-permute-start | bytes 1572872 | tf_op jit(solution)/shard_map/ppermute | solution.py:558
  14.6 52.0 %collective-permute-start.3 = (bf16[4,256,256]{2,1,0:T(8,128)(2,1)}, bf16[4,256,256]{2,1,0:T(8,128)(2,1)S(1)}, u32[]{:S(2)}, u32[]{:S(2)}) collective-permute-start(bf16[4,256,256]{2,1,0:T(8,128)(2,1)} %get-tuple-element.54), channel_id=1, source_target_pairs={{0,4},{4,8},{8,12},{12,16},{16,20},{20,24},{24,28},{1,5},{5,9},{9,... | collective-permute-start | bytes 1572872 | tf_op jit(solution)/shard_map/ppermute | solution.py:558
  19.2 84.2 %collective-permute-start = (bf16[4,256,256]{2,1,0:T(8,128)(2,1)}, bf16[4,256,256]{2,1,0:T(8,128)(2,1)S(1)}, u32[]{:S(2)}, u32[]{:S(2)}) collective-permute-start(bf16[4,256,256]{2,1,0:T(8,128)(2,1)} %get-tuple-element.30), channel_id=1, source_target_pairs={{0,4},{4,8},{8,12},{12,16},{16,20},{20,24},{24,28},{1,5},{5,9},{9,... | collective-permute-start | bytes 1572872 | tf_op jit(solution)/shard_map/ppermute | solution.py:558
  24.1 79.4 %collective-permute-start.1 = (bf16[4,256,256]{2,1,0:T(8,128)(2,1)}, bf16[4,256,256]{2,1,0:T(8,128)(2,1)}, u32[]{:S(2)}, u32[]{:S(2)}) collective-permute-start(bf16[4,256,256]{2,1,0:T(8,128)(2,1)} %get-tuple-element.31), channel_id=1, source_target_pairs={{4,0},{8,4},{12,8},{16,12},{20,16},{24,20},{28,24},{5,1},{9,5},{13... | collective-permute-start | bytes 1572872 | tf_op jit(solution)/shard_map/ppermute | solution.py:558
  25.4 74.5 %collective-permute-start.6 = (bf16[4,256,256]{2,1,0:T(8,128)(2,1)}, bf16[4,256,256]{2,1,0:T(8,128)(2,1)}, u32[]{:S(2)}, u32[]{:S(2)}) collective-permute-start(bf16[4,256,256]{2,1,0:T(8,128)(2,1)} %get-tuple-element.41), channel_id=1, source_target_pairs={{0,4},{4,8},{8,12},{12,16},{16,20},{20,24},{24,28},{1,5},{5,9},{9,... | collective-permute-start | bytes 1572872 | tf_op jit(solution)/shard_map/ppermute | solution.py:558
  47.6 2.2 %copy-start.2 = (bf16[1,32,256,256]{3,2,1,0:T(8,128)(2,1)S(1)}, bf16[1,32,256,256]{3,2,1,0:T(8,128)(2,1)}, u32[]{:S(2)}) copy-start(bf16[1,32,256,256]{3,2,1,0:T(8,128)(2,1)} %movie.1) | copy-start | bytes 12582916
  49.8 33.3 %copy-start.22 = (f32[1,256]{1,0:T(1,128)S(1)}, f32[1,256]{1,0:T(1,128)}, u32[]{:S(2)}) copy-start(f32[1,256]{1,0:T(1,128)} %param.16) | copy-start | bytes 3076
  59.9 2.0 %copy-start = (bf16[32,256,256]{2,1,0:T(8,128)(2,1)}, bf16[32,256,256]{2,1,0:T(8,128)(2,1)S(1)}, u32[]{:S(2)}) copy-start(bf16[32,256,256]{2,1,0:T(8,128)(2,1)S(1)} %get-tuple-element.29.own) | copy-start | bytes 12582916
  61.9 2.0 %copy-start.3 = (bf16[32,256,256]{2,1,0:T(8,128)(2,1)}, bf16[32,256,256]{2,1,0:T(8,128)(2,1)S(1)}, u32[]{:S(2)}) copy-start(bf16[32,256,256]{2,1,0:T(8,128)(2,1)S(1)} %get-tuple-element.33.own) | copy-start | bytes 12582916
  63.9 0.6 copy-start.17
  64.5 0.8 copy-start.9
  65.3 34.5 %collective-permute-start.7 = (bf16[4,256,256]{2,1,0:T(8,128)(2,1)}, bf16[4,256,256]{2,1,0:T(8,128)(2,1)}, u32[]{:S(2)}, u32[]{:S(2)}) collective-permute-start(bf16[4,256,256]{2,1,0:T(8,128)(2,1)} %get-tuple-element.42), channel_id=1, source_target_pairs={{4,0},{8,4},{12,8},{16,12},{20,16},{24,20},{28,24},{5,1},{9,5},{13... | collective-permute-start | bytes 1572872 | tf_op jit(solution)/shard_map/ppermute | solution.py:558
  66.6 0.8 copy-start.11
  67.4 1.0 copy-start.10
  68.5 1.0 copy-start.12
  69.5 0.9 copy-start.14
  70.4 25.4 %copy-start.5 = (bf16[256,512]{1,0:T(8,128)(2,1)S(1)}, bf16[256,512]{1,0:T(8,128)(2,1)}, u32[]{:S(2)}) copy-start(bf16[256,512]{1,0:T(8,128)(2,1)} %constant.24.clone.band) | copy-start | bytes 786436
  72.4 1.0 copy-start.7
  74.8 21.1 %copy-start.1 = (bf16[32,256,256]{2,1,0:T(8,128)(2,1)S(1)}, bf16[32,256,256]{2,1,0:T(8,128)(2,1)}, u32[]{:S(2)}) copy-start(bf16[32,256,256]{2,1,0:T(8,128)(2,1)} %copy-done) | copy-start | bytes 12582916
  75.7 3.2 %collective-permute-start.5 = (f32[40,256]{1,0:T(8,128)S(1)}, f32[40,256]{1,0:T(8,128)S(1)}, u32[]{:S(2)}, u32[]{:S(2)}) collective-permute-start(f32[40,256]{1,0:T(8,128)S(1)} %pad_maximum_fusion), channel_id=1, source_target_pairs={{1,0},{2,1},{3,2},{5,4},{6,5},{7,6},{9,8},{10,9},{11,10},{13,12},{... | collective-permute-start | bytes 122888 | tf_op jit(solution)/shard_map/ppermute | solution.py:568
  78.9 7.0 %collective-permute-start.4 = (f32[40,256]{1,0:T(8,128)S(1)}, f32[40,256]{1,0:T(8,128)S(1)}, u32[]{:S(2)}, u32[]{:S(2)}) collective-permute-start(f32[40,256]{1,0:T(8,128)S(1)} %pad_maximum_fusion), channel_id=1, source_target_pairs={{0,1},{1,2},{2,3},{4,5},{5,6},{6,7},{8,9},{9,10},{10,11},{12,13},{... | collective-permute-start | bytes 122888 | tf_op jit(solution)/shard_map/ppermute | solution.py:567
  86.7 2.2 %copy-start.4 = (bf16[32,256,256]{2,1,0:T(8,128)(2,1)S(1)}, bf16[32,256,256]{2,1,0:T(8,128)(2,1)}, u32[]{:S(2)}) copy-start(bf16[32,256,256]{2,1,0:T(8,128)(2,1)} %copy-done.3) | copy-start | bytes 12582916
  88.8 1.2 copy-start.8
  90.1 0.9 copy-start.16
  103.5 38.8 %copy-start.20 = (f32[1,128]{1,0:T(1,128)S(1)}, f32[1,128]{1,0:T(1,128)}, u32[]{:S(2)}) copy-start(f32[1,128]{1,0:T(1,128)} %slow.1) | copy-start | bytes 1540
  103.5 38.8 %copy-start.21 = (f32[1,128]{1,0:T(1,128)S(1)}, f32[1,128]{1,0:T(1,128)}, u32[]{:S(2)}) copy-start(f32[1,128]{1,0:T(1,128)} %fast.1) | copy-start | bytes 1540
  107.9 34.3 %all-to-all-start.1 = ((bf16[8,32,1024]{2,1,0:T(8,128)(2,1)}), bf16[8,32,1024]{2,1,0:T(8,128)(2,1)S(1)}, u32[]{:S(2)}, u32[]{:S(2)}) async-start(bf16[8,32,1024]{2,1,0:T(8,128)(2,1)} %bitcast.13), calls=%async_computation.1 | async-start | bytes 1048576 | tf_op jit(solution)/shard_map/all_to_all | solution.py:579
where the time goes:
time: 145 us
  starting transfers between devices  51.2 us (35%)
  Pallas kernels  35.5 us (24%)
  waiting for transfers between devices  33.2 us (23%)
  local copies, waits for them, and re-layouts  21.8 us (15%)
  other arithmetic  1.85 us (1%)
    all_to_all x1, starting transfers between devices, on_device(): lax.all_to_all(gradient, 'pix', split_axis=0, concat_axis=0, tiled=True)  19.7 us
    all_to_all x1, waiting for transfers between devices, on_device(): lax.all_to_all(outbox, 'pix', split_axis=0, concat_axis=0, tiled=True)  16.8 us
    unnamed x46, local copies, waits for them, and re-layouts  16.8 us
    ppermute x3, starting transfers between devices, exchange(): lax.ppermute(cut[0], 'pix', pix_up)  14.8 us
    all_to_all x1, waiting for transfers between devices, on_device(): lax.all_to_all(gradient, 'pix', split_axis=0, concat_axis=0, tiled=True)  14.5 us
    pallas_call x3, Pallas kernels, call(): pl.pallas_call(kernel, in_specs=specs, out_specs=[ANY] + [VMEM] * (len(ou...  12 us
    pallas_call x1, Pallas kernels, make_residual(): pl.pallas_call(residual_kernel, out_shape=(jax.ShapeDtypeStruct((rows, sl...  10.1 us
    all_to_all x1, starting transfers between devices, on_device(): lax.all_to_all(outbox, 'pix', split_axis=0, concat_axis=0, tiled=True)  7.28 us
  transfers between devices with their start and end apart: 10, of which 3 were waited for; matrix products, arithmetic and copies ran while one was open for 2% of the time, Pallas kernels for 19%

commit v1 on v0

--- a/solution.py
+++ b/solution.py
@@ -24,7 +24,7 @@
 F32 = jnp.float32
 BF16 = jnp.bfloat16
 MIB = 1 << 20
-ANY = pl.BlockSpec(memory_space=pl.ANY)
+HBM = pl.BlockSpec(memory_space=pltpu.HBM)
 VMEM = pl.BlockSpec(memory_space=pltpu.VMEM)
 
 
@@ -45,7 +45,17 @@
     return jnp.dot(a, b, preferred_element_type=F32)
 
 
-def outbox_kernel(capacity, stripe, column, foot, traces, outbox):
+def outbox_kernel(capacity, *refs):
+    sources, outbox, places, sems = refs[0:4], refs[4], refs[5:9], refs[9]
+    copies = [
+        pltpu.make_async_copy(source, place, sems.at[k])
+        for k, (source, place) in enumerate(zip(sources, places))
+    ]
+    for copy in copies:
+        copy.start()
+    for copy in copies:
+        copy.wait()
+    stripe, column, foot, traces = places
     slots = outbox.shape[0]
     count, tiles = foot.shape
     frames = traces.shape[1]
@@ -77,13 +87,17 @@
     count, tiles = foot.shape
     frames = traces.shape[1]
     width = 3 * frames + tiles + 2 * RAD * FOOT + LANES
+    args = (stripe, column, foot, traces)
     return pl.pallas_call(
         functools.partial(outbox_kernel, capacity),
+        in_specs=[HBM] * len(args),
         out_shape=jax.ShapeDtypeStruct((slots, width), BF16),
-        compiler_params=params(),
+        scratch_shapes=[pltpu.VMEM(a.shape, a.dtype) for a in args]
+        + [pltpu.SemaphoreType.DMA((len(args),))],
+        compiler_params=params(56),
         cost_estimate=COST,
         name="outbox",
-    )(stripe, column, foot, traces)
+    )(*args)
 
 
 def spread(block, col):
@@ -128,51 +142,104 @@
     return jnp.sum(part.T, axis=0, keepdims=True) / (frames - 1)
 
 
+def lag_table(size):
+    shape = (size, size)
+    return lax.broadcasted_iota(jnp.int32, shape, 1) - lax.broadcasted_iota(jnp.int32, shape, 0)
+
+
 def change_matrix(frames):
-    earlier, later = np.arange(frames)[:, None], np.arange(frames)[None, :]
-    steps = (earlier == later + 1).astype(np.float32) - (earlier == later)
-    return jnp.asarray(np.where(later < frames - 1, steps, 0.0).astype(ml_dtypes.bfloat16))
-
-
-def residual_kernel(inbox, movie, change, foot_rows, residual, noise):
+    lag = lag_table(frames)
+    steps = jnp.where(lag == -1, 1.0, 0.0) - jnp.where(lag == 0, 1.0, 0.0)
+    later = lax.broadcasted_iota(jnp.int32, lag.shape, 1)
+    return jnp.where(later < frames - 1, steps, 0.0).astype(BF16)
+
+
+def residual_kernel(
+    inbox, movie, foot_rows, residual, noise, change, movie_slots, foot_slots, left_slots, sems
+):
     rows, _, frames = movie.shape[1:]
+    groups = rows // PER
+    change[...] = change_matrix(frames)
+
+    def fetch(g, slot):
+        rows_g = pl.ds(g * PER, PER)
+        return pltpu.make_async_copy(movie.at[0, rows_g], movie_slots.at[slot], sems.at[0, slot])
+
+    def sends(g, slot):
+        rows_g = pl.ds(g * PER, PER)
+        return (
+            pltpu.make_async_copy(foot_slots.at[slot], foot_rows.at[rows_g], sems.at[1, slot]),
+            pltpu.make_async_copy(left_slots.at[slot], residual.at[rows_g], sems.at[2, slot]),
+        )
+
+    fetch(0, 0).start()
 
     def group(g, carry):
+        slot = lax.rem(g, 2)
+
+        @pl.when(g + 1 < groups)
+        def _():
+            fetch(g + 1, 1 - slot).start()
+
+        fetch(g, slot).wait()
+
+        @pl.when(g >= 2)
+        def _():
+            for copy in sends(g - 2, slot):
+                copy.wait()
+
         noises = []
         for q, row in enumerate(tile_rows(inbox, 0, g, frames)):
-            y = g * PER + q
-            foot_rows[y] = row
-            left = (movie[0, y].astype(F32) - model_row(row, inbox, 0, frames)).astype(BF16)
-            residual[y] = left
+            foot_slots[slot, q] = row
+            left = movie_slots[slot, q].astype(F32) - model_row(row, inbox, 0, frames)
+            left = left.astype(BF16)
+            left_slots[slot, q] = left
             noises.append(noise_row(left, change[...]))
         noise[g] = jnp.concatenate(noises, axis=0)
+        for copy in sends(g, slot):
+            copy.start()
         return carry
 
-    lax.fori_loop(0, rows // PER, group, 0)
-
-
-def make_residual(inbox, movie, change):
+    lax.fori_loop(0, groups, group, 0)
+    for g in (groups - 2, groups - 1):
+        for copy in sends(g, g % 2):
+            copy.wait()
+
+
+def make_residual(inbox, movie):
     slots = inbox.shape[0]
     rows, cols, frames = movie.shape[1:]
-    foot_rows, residual, noise = pl.pallas_call(
+    return pl.pallas_call(
         residual_kernel,
+        in_specs=[VMEM, HBM],
+        out_specs=[HBM, HBM, VMEM],
         out_shape=(
             jax.ShapeDtypeStruct((rows, slots, cols), BF16),
             jax.ShapeDtypeStruct((rows, cols, frames), BF16),
             jax.ShapeDtypeStruct((rows // PER, PER, cols), F32),
         ),
-        compiler_params=params(),
+        scratch_shapes=[
+            pltpu.VMEM((frames, frames), BF16),
+            pltpu.VMEM((2, PER, cols, frames), BF16),
+            pltpu.VMEM((2, PER, slots, cols), BF16),
+            pltpu.VMEM((2, PER, cols, frames), BF16),
+            pltpu.SemaphoreType.DMA((3, 2)),
+        ],
+        compiler_params=params(44),
         cost_estimate=COST,
         name="residual",
-    )(inbox, movie, change)
-    return foot_rows, residual, noise.reshape(rows, cols)
-
-
-def near_kernel(inbox, movie_next, movie_prev, change, foot_rows, residual, noise):
+    )(inbox, movie)
+
+
+def near_kernel(inbox, movie_next, movie_prev, own_noise, foot_rows, residual, noise):
     frames = movie_next.shape[2]
+    groups = own_noise.shape[0]
     own = FOOT // PER
-    for side, (block, movie) in enumerate(
-        ((own, movie_next), (own + 2 * RAD // PER - 1, movie_prev))
+    change = change_matrix(frames)
+    for g in range(groups):
+        noise[NEAR + g * PER : NEAR + (g + 1) * PER, :] = own_noise[g]
+    for side, (block, movie, first) in enumerate(
+        ((own, movie_next, 0), (own + 2 * RAD // PER - 1, movie_prev, NEAR + groups * PER))
     ):
         for q, row in enumerate(tile_rows(inbox, 1 + side, block, frames)):
             y = side * NEAR + q
@@ -180,48 +247,67 @@
             left = movie[q].astype(F32) - model_row(row, inbox, 1 + side, frames)
             left = left.astype(BF16)
             residual[y] = left
-            noise[y : y + 1, :] = noise_row(left, change[...])
-
-
-def make_near(inbox, movie_next, movie_prev, change):
+            noise[first + q : first + q + 1, :] = noise_row(left, change)
+
+
+def make_near(inbox, movie_next, movie_prev, noise):
     slots = inbox.shape[0]
+    groups, per, _ = noise.shape
     cols, frames = movie_next.shape[1:]
     return pl.pallas_call(
         near_kernel,
         out_shape=(
             jax.ShapeDtypeStruct((2 * NEAR, slots, cols), BF16),
             jax.ShapeDtypeStruct((2 * NEAR, cols, frames), BF16),
-            jax.ShapeDtypeStruct((2 * NEAR, cols), F32),
+            jax.ShapeDtypeStruct((2 * NEAR + groups * per, cols), F32),
         ),
         compiler_params=params(),
         cost_estimate=COST,
         name="near",
-    )(inbox, movie_next, movie_prev, change)
-
-
-def outer_kernel(inbox, *models):
-    frames = models[0].shape[2]
-    own = FOOT // PER
-    groups = RAD // PER
-    for piece, model in enumerate(models, 1):
-        for side, block in enumerate((own + piece, own + 2 * groups - 1 - piece)):
-            for q, row in enumerate(tile_rows(inbox, 1 + side, block, frames)):
-                model[side * PER + q] = model_row(row, inbox, 1 + side, frames)
-
-
-def make_outer_models(inbox, cols, frames):
-    piece = jax.ShapeDtypeStruct((2 * PER, cols, frames), F32)
+    )(inbox, movie_next, movie_prev, noise)
+
+
+def outer_kernel(inbox, model):
+    frames = model.shape[2]
+    first = (FOOT + NEAR) // PER
+    groups = (RAD - NEAR) // PER
+    for side in range(2):
+        for g in range(groups):
+            k = side * groups + g
+            for q, row in enumerate(tile_rows(inbox, 1 + side, first + k, frames)):
+                model[k * PER + q] = model_row(row, inbox, 1 + side, frames)
+
+
+def make_outer_model(inbox, cols, frames):
     return pl.pallas_call(
         outer_kernel,
-        out_shape=(piece,) * (RAD // PER - 1),
+        out_shape=jax.ShapeDtypeStruct((2 * (RAD - NEAR), cols, frames), F32),
         compiler_params=params(),
         cost_estimate=COST,
-        name="outer_models",
+        name="outer_model",
     )(inbox)
 
 
-def weights_kernel(taps, part, own, near, scale, band, out, out_next, out_prev):
+def weights_kernel(
+    taps, own, near, noise, noise_before, noise_after, out, out_next, out_prev,
+    own_slots, scale, band, sems,
+):
     rows, slots, cols = own.shape
+    part = own_slots.shape[2]
+    count = slots // part
+
+    def fetch(i, slot):
+        these = pl.ds(pl.multiple_of(i * part, part), part)
+        return pltpu.make_async_copy(own.at[:, these, :], own_slots.at[slot], sems.at[slot])
+
+    fetch(0, 0).start()
+    pooled = (noise_before[...] + 2.0 * noise[...] + noise_after[...]) / 4.0
+    scale[...] = 1.0 / jnp.sqrt(pooled + noise_eps)
+    lag = jnp.abs(lag_table(cols))
+    table = jnp.zeros(lag.shape, F32)
+    for k in range(GR + 1):
+        table = jnp.where(lag == k, taps[GR + k], table)
+    band[...] = table.astype(BF16)
 
     def across(foot, inv):
         scaled = (foot.astype(F32) * inv[:, None, :]).astype(BF16)
@@ -229,8 +315,15 @@
         return dot(scaled.reshape(count * part, cols), band[...]).reshape(count, part, cols)
 
     def some(i, carry):
+        slot = lax.rem(i, 2)
+
+        @pl.when(i + 1 < count)
+        def _():
+            fetch(i + 1, 1 - slot).start()
+
+        fetch(i, slot).wait()
         these = pl.ds(pl.multiple_of(i * part, part), part)
-        blurred = across(own[:, these, :], scale[NEAR : NEAR + rows])
+        blurred = across(own_slots[slot], scale[NEAR : NEAR + rows])
         for r in range(rows):
             total = taps[GR] * blurred[r]
             for k in range(1, GR + 1):
@@ -254,26 +347,30 @@
             out_prev[a, these, :] = total.astype(BF16)
         return carry
 
-    lax.fori_loop(0, slots // part, some, 0)
-
-
-def make_weights(foot_rows, near_rows, scale):
+    lax.fori_loop(0, count, some, 0)
+
+
+def make_weights(foot_rows, near_rows, noises):
     rows, slots, cols = foot_rows.shape
-    taps = tap_values()
-    lag = np.arange(cols)[:, None] - np.arange(cols)[None, :]
-    band = np.where(np.abs(lag) <= GR, taps[np.clip(lag + GR, 0, 2 * GR)], 0.0)
-    band = jnp.asarray(band.astype(ml_dtypes.bfloat16))
+    part = 32
     return pl.pallas_call(
-        functools.partial(weights_kernel, [float(t) for t in taps], 32),
+        functools.partial(weights_kernel, [float(t) for t in tap_values()]),
+        in_specs=[HBM] + [VMEM] * (1 + len(noises)),
         out_shape=(
             jax.ShapeDtypeStruct((rows, slots, cols), BF16),
             jax.ShapeDtypeStruct((GR, slots, cols), BF16),
             jax.ShapeDtypeStruct((GR, slots, cols), BF16),
         ),
-        compiler_params=params(),
+        scratch_shapes=[
+            pltpu.VMEM((2, rows, part, cols), BF16),
+            pltpu.VMEM(noises[0].shape, F32),
+            pltpu.VMEM((cols, cols), BF16),
+            pltpu.SemaphoreType.DMA((2,)),
+        ],
+        compiler_params=params(32),
         cost_estimate=COST,
         name="weights",
-    )(foot_rows, near_rows, scale, band)
+    )(foot_rows, near_rows, *noises)
 
 
 def annulus_group(g, own, leaving, entering, weight, gain, band, column, total, outgoing):
@@ -319,116 +416,102 @@
         ref[:, h * LANES : (h + 1) * LANES] = value
 
 
-def subtracted(movie, model, first):
-    return [(movie[r].astype(F32) - model[first + r]).astype(BF16) for r in range(PER)]
-
-
 def sender(outgoing, background, sems):
-    def send(g, slot):
+    def send(g):
         return pltpu.make_async_copy(
-            outgoing.at[g], background.at[0, pl.ds(g * PER, PER)], sems.at[slot]
+            outgoing.at[g], background.at[0, pl.ds(g * PER, PER)], sems.at[g]
         )
 
     return send
 
 
-def middle_kernel(
-    own, near, weight, gain, band, background, upper, lower, total, outgoing, sems
-):
+def tables(gain):
+    cols = gain.shape[1]
+    band = jnp.where(jnp.abs(lag_table(cols)) <= RAD, 1.0, 0.0).astype(BF16)
+    return (
+        jnp.broadcast_to(gain[...], (LANES, cols)).T / (8.0 * RAD),
+        jnp.concatenate([band, band], axis=1),
+    )
+
+
+def middle_kernel(own, near, weight, gain, background, upper, lower, total, outgoing, sems):
     rows, cols, frames = own.shape
-    first, last = RAD // PER - 1, (rows - RAD) // PER + 1
+    groups = range((RAD - NEAR) // PER, (rows - RAD + NEAR) // PER)
     send = sender(outgoing, background, sems)
-    column = add_rows([jnp.zeros((cols, LANES), F32)] * (frames // LANES), [
-        near[NEAR + r] for r in range(NEAR)
-    ])
-    column = add_rows(column, [own[r] for r in range(RAD + NEAR)])
+    gains, band = tables(gain)
+    column = [jnp.zeros((cols, LANES), F32)] * (frames // LANES)
+    column = add_rows(column, [near[NEAR + r] for r in range(NEAR)])
+    column = add_rows(column, [own[r] for r in range(RAD)])
     put(upper, column)
-    column = add_rows(column, [own[RAD + NEAR + r] for r in range(PER)])
+    column = add_rows(column, [own[RAD + r] for r in range(2 * RAD - NEAR - RAD)])
     grown = jnp.zeros(total.shape, F32)
-    for k, g in enumerate(range(first, last)):
+    for g in groups:
         y = g * PER
         column, grown, _ = annulus_group(
             g,
             own,
-            (lambda q: near[NEAR + q]) if g == first else (lambda q: own[y - RAD + q]),
-            (lambda q: near[q]) if g == last - 1 else (lambda q: own[y + RAD + q]),
-            weight, gain[...], band[...], column, grown, outgoing,
+            (lambda q: near[NEAR + y - RAD + NEAR + q])
+            if y < RAD
+            else (lambda q: own[y - RAD + q]),
+            (lambda q: near[y + RAD - rows + q])
+            if y + RAD >= rows
+            else (lambda q: own[y + RAD + q]),
+            weight, gains, band, column, grown, outgoing,
         )
-        send(g, k).start()
+        send(g).start()
     put(lower, column)
     total[...] = grown
-    for k, g in enumerate(range(first, last)):
-        send(g, k).wait()
-
-
-def mid_kernel(
-    own, near, movie_prev, movie_next, model, weight, gain, band, before, upper, lower, total,
-    background, new_upper, new_lower, new_total, outgoing, sems,
-):
-    del before
-    rows = own.shape[0]
-    low, high = RAD // PER - 2, (rows - RAD) // PER + 1
-    send = sender(outgoing, background, sems)
-    above, below = subtracted(movie_prev, model, PER), subtracted(movie_next, model, 0)
-    column = add_rows(halves(upper), above)
-    put(new_upper, add_rows(column, [own[RAD + r] for r in range(PER)], -1.0))
-    y = low * PER
-    _, grown, _ = annulus_group(
-        low, own, lambda q: above[q], lambda q: own[y + RAD + q],
-        weight, gain[...], band[...], column, total[...], outgoing,
-    )
-    send(low, 0).start()
-    z = high * PER
-    column, grown, _ = annulus_group(
-        high, own, lambda q: own[z - RAD + q], lambda q: below[q],
-        weight, gain[...], band[...], halves(lower), grown, outgoing,
-    )
-    send(high, 1).start()
-    put(new_lower, column)
-    new_total[...] = grown
-    send(low, 0).wait()
-    send(high, 1).wait()
-
-
-def end_kernel(
-    own, movie_prev, movie_next, model, weight, weight_next, weight_prev, gain, band, before,
+    for g in groups:
+        send(g).wait()
+
+
+def ends_kernel(
+    own, movie_prev, movie_next, model, weight, weight_next, weight_prev, gain, before,
     upper, lower, total, background, gradient, outgoing, sems,
 ):
     del before
     rows, _, frames = own.shape
-    low, high = 0, rows // PER - 1
+    outer = RAD - NEAR
+    count = outer // PER
     send = sender(outgoing, background, sems)
-    above, below = subtracted(movie_prev, model, PER), subtracted(movie_next, model, 0)
-    _, grown, low_dets = annulus_group(
-        low, own, lambda q: above[q], lambda q: own[RAD + q],
-        weight, gain[...], band[...], add_rows(halves(upper), above), total[...], outgoing,
-    )
-    send(low, 0).start()
-    z = high * PER
-    _, grown, high_dets = annulus_group(
-        high, own, lambda q: own[z - RAD + q], lambda q: below[q],
-        weight, gain[...], band[...], halves(lower), grown, outgoing,
-    )
-    send(high, 1).start()
-    for at, edge, dets in ((2, weight_next, high_dets[PER - GR :]), (3, weight_prev, low_dets[:GR])):
+    gains, band = tables(gain)
+    above, below = [
+        [(movie[r].astype(F32) - model[first + r]).astype(BF16) for r in range(outer)]
+        for movie, first in ((movie_prev, outer), (movie_next, 0))
+    ]
+    high, low = add_rows(halves(upper), above), halves(lower)
+    grown = total[...]
+    dets = {}
+    for k in range(count):
+        y, z = k * PER, rows - outer + k * PER
+        high, grown, dets[y] = annulus_group(
+            y // PER, own, lambda q: above[y + q], lambda q: own[y + RAD + q],
+            weight, gains, band, high, grown, outgoing,
+        )
+        send(y // PER).start()
+        low, grown, dets[z] = annulus_group(
+            z // PER, own, lambda q: own[z - RAD + q], lambda q: below[k * PER + q],
+            weight, gains, band, low, grown, outgoing,
+        )
+        send(z // PER).start()
+    edges = ((2, weight_next, dets[rows - PER][PER - GR :]), (3, weight_prev, dets[0][:GR]))
+    for at, edge, parts in edges:
         value = dot(
-            jnp.concatenate([edge[a] for a in range(GR)], axis=1), jnp.concatenate(dets, axis=0)
+            jnp.concatenate([edge[a] for a in range(GR)], axis=1), jnp.concatenate(parts, axis=0)
         )
         gradient[:, at * frames : (at + 1) * frames] = value.astype(BF16)
-    upper_half = grown.astype(BF16)
-    gradient[:, 0:frames] = upper_half
-    gradient[:, frames : 2 * frames] = (grown - upper_half.astype(F32)).astype(BF16)
-    send(low, 0).wait()
-    send(high, 1).wait()
-
-
-def make_annulus(own, near, movies, models, weights, gain):
+    coarse = grown.astype(BF16)
+    gradient[:, 0:frames] = coarse
+    gradient[:, frames : 2 * frames] = (grown - coarse.astype(F32)).astype(BF16)
+    for k in range(count):
+        send(k).wait()
+        send(rows // PER - 1 - k).wait()
+
+
+def make_annulus(own, near, outer_prev, outer_next, model, weights, gain):
     rows, cols, frames = own.shape
     weight, weight_next, weight_prev = weights
     slots = weight.shape[1]
-    lag = np.arange(cols)[:, None] - np.arange(cols)[None, :]
-    band = (np.abs(lag) <= RAD).astype(ml_dtypes.bfloat16)
-    band = jnp.asarray(np.concatenate([band, band], axis=1))
     background = jax.ShapeDtypeStruct((1, rows, cols, frames), BF16)
     column = jax.ShapeDtypeStruct((cols, frames), F32)
     total = jax.ShapeDtypeStruct((slots, frames), F32)
@@ -437,11 +520,11 @@
     def call(kernel, name, args, outs, done):
         specs = [VMEM] * len(args)
         if done is not None:
-            specs[done] = ANY
+            specs[done] = HBM
         return pl.pallas_call(
             kernel,
             in_specs=specs,
-            out_specs=[ANY] + [VMEM] * (len(outs) - 1),
+            out_specs=[HBM] + [VMEM] * (len(outs) - 1),
             out_shape=outs,
             scratch_shapes=[
                 pltpu.VMEM((rows // PER, PER, cols, frames), BF16),
@@ -454,19 +537,14 @@
         )(*args)
 
     done, upper, lower, grown = call(
-        middle_kernel, "annulus_middle", (own, near, weight, gain, band),
+        middle_kernel, "annulus_middle", (own, near, weight, gain),
         (background, column, column, total), None,
     )
-    done, upper, lower, grown = call(
-        mid_kernel, "annulus_mid",
-        (own, near, *movies[0], models[0], weight, gain, band, done, upper, lower, grown),
-        (background, column, column, total), 8,
-    )
     return call(
-        end_kernel, "annulus_end",
-        (own, *movies[1], models[1], weight, weight_next, weight_prev, gain, band, done, upper,
+        ends_kernel, "annulus_ends",
+        (own, outer_prev, outer_next, model, weight, weight_next, weight_prev, gain, done, upper,
          lower, grown),
-        (background, gradient), 9,
+        (background, gradient), 8,
     )
 
 
@@ -546,35 +624,30 @@
 
     stripe_row = stripe.reshape(1, count)
     outbox = make_outbox(stripe_row, column, footprints[0], traces[0], capacity, slots)
-    cuts = [
-        (movie[0, rows - (k + 1) * PER : rows - k * PER], movie[0, k * PER : (k + 1) * PER])
-        for k in range(RAD // PER)
-    ]
-
-    cuts[1:], outbox = lax.optimization_barrier((cuts[1:], outbox))
+    frames_in, outbox = lax.optimization_barrier((movie, outbox))
     inbox = lax.all_to_all(outbox, "pix", split_axis=0, concat_axis=0, tiled=True)
 
     def exchange(cut):
         return (lax.ppermute(cut[0], "pix", pix_up), lax.ppermute(cut[1], "pix", pix_down))
 
-    near_prev, near_next = exchange(cuts[0])
-    mid, far = exchange(cuts[1]), exchange(cuts[2])
-
-    change = change_matrix(frames)
-    foot_rows, residual, noise = make_residual(inbox, movie, change)
-    near_rows, near_residual, near_noise = make_near(inbox, near_next, near_prev, change)
-    noise = jnp.concatenate([near_noise[:NEAR], noise, near_noise[NEAR:]], axis=0)
-    noise_before = lax.ppermute(noise, "plane", plane_up)
-    noise_after = lax.ppermute(noise, "plane", plane_down)
-    pooled = (noise_before + 2.0 * noise + noise_after) / 4.0
-    scale = 1.0 / jnp.sqrt(pooled + noise_eps)
-
-    weights = make_weights(foot_rows, near_rows, scale)
-    models = make_outer_models(inbox, cols, frames)
-
-    gain = jnp.broadcast_to((annulus_gain[0] / (8.0 * RAD))[:, None], (cols, LANES))
+    near = exchange((frames_in[0, rows - NEAR :], frames_in[0, :NEAR]))
+    cut, near = lax.optimization_barrier(
+        ((frames_in[0, rows - RAD : rows - NEAR], frames_in[0, NEAR:RAD]), near)
+    )
+    outer_prev, outer_next = exchange(cut)
+    near_prev, near_next = near
+
+    foot_rows, residual, noise = make_residual(inbox, movie)
+    near_rows, near_residual, noise = make_near(inbox, near_next, near_prev, noise)
+    noises = (
+        noise,
+        lax.ppermute(noise, "plane", plane_up),
+        lax.ppermute(noise, "plane", plane_down),
+    )
+    weights = make_weights(foot_rows, near_rows, noises)
+    model = make_outer_model(inbox, cols, frames)
     background, gradient = make_annulus(
-        residual, near_residual, (mid, far), models, weights, gain
+        residual, near_residual, outer_prev, outer_next, model, weights, annulus_gain
     )
     home = lax.all_to_all(gradient, "pix", split_axis=0, concat_axis=0, tiled=True)
     foot_f = footprints[0].astype(F32)

time: 145 us -> 132 us (0.910)
  waiting for transfers between devices: 33.2 us -> 56.8 us
  starting transfers between devices: 51.2 us -> 32.4 us
  local copies, waits for them, and re-layouts: 21.8 us -> 5.97 us
  other arithmetic: 1.85 us -> 0.14 us
    ppermute x3 -> x2, waiting for transfers between devices: 0.01 us -> 41.6 us  [exchange(): lax.ppermute(cut[0], 'pix', pix_up)]
    all_to_all x1, waiting for transfers between devices: 16.8 us -> 0.01 us  [on_device(): lax.all_to_all(outbox, 'pix', split_axis=0, concat_axis=0, tiled=True)]
    unnamed x46 -> x20, local copies, waits for them, and re-layouts: 16.8 us -> 1.63 us
    all_to_all x1, starting transfers between devices: 19.7 us -> 11.4 us  [on_device(): lax.all_to_all(gradient, 'pix', split_axis=0, concat_axis=0, tiled=True)]
    ppermute x3 -> x2, starting transfers between devices: 14.8 us -> 8.4 us  [exchange(): lax.ppermute(cut[0], 'pix', pix_up)]
    ppermute x2, starting transfers between devices: 5.57 us -> 2.76 us  [the longest x1 1.47 us: on_device(): lax.ppermute(noise, 'plane', plane_down)]
    ppermute x3 -> x2, starting transfers between devices: 3.85 us -> 2.58 us  [exchange(): lax.ppermute(cut[1], 'pix', pix_down)]
    squeeze x1 -> x2, local copies, waits for them, and re-layouts: 3.63 us -> 4.34 us  [the longest x1 3.07 us: on_device(): frames_in[0, NEAR:RAD]]
  transfers between devices with their start and end apart: 10 -> 8, of which waited for: 3 -> 4; matrix products, arithmetic and copies ran while one was open for 2% -> 3% of each run, Pallas kernels for 19% -> 19%
where the time goes in v1:
time: 132 us; the launch traced here: 131 us
  waiting for transfers between devices  56.8 us (43%)
  Pallas kernels  35.2 us (27%)
  starting transfers between devices  32.4 us (25%)
  local copies, waits for them, and re-layouts  5.97 us (5%)
    ppermute x2, waiting for transfers between devices, exchange(): lax.ppermute(cut[0], 'pix', pix_up)  41.6 us
    all_to_all x1, waiting for transfers between devices, on_device(): lax.all_to_all(gradient, 'pix', split_axis=0, concat_axis=0, tiled=True)  14.5 us
    pallas_call x1, Pallas kernels, make_residual(): pl.pallas_call(residual_kernel, in_specs=[VMEM, HBM], out_specs=[HBM, HBM...  11.9 us
    all_to_all x1, starting transfers between devices, on_device(): lax.all_to_all(gradient, 'pix', split_axis=0, concat_axis=0, tiled=True)  11.4 us
    pallas_call x2, Pallas kernels, call(): pl.pallas_call(kernel, in_specs=specs, out_specs=[HBM] + [VMEM] * (len(ou...  8.53 us
    ppermute x2, starting transfers between devices, exchange(): lax.ppermute(cut[0], 'pix', pix_up)  8.4 us
    all_to_all x1, starting transfers between devices, on_device(): lax.all_to_all(outbox, 'pix', split_axis=0, concat_axis=0, tiled=True)  7.29 us
    pallas_call x1, Pallas kernels, make_weights(): pl.pallas_call(functools.partial(weights_kernel, [float(t) for t in tap_v...  5.25 us
  transfers between devices with their start and end apart: 8, of which 4 were waited for; matrix products, arithmetic and copies ran while one was open for 3% of the time, Pallas kernels for 19%

profile of v1, /device:TPU:0, one launch (start us, length us, event | category | flops | bytes accessed | tf_op | source)
XLA Modules:
  0.0 131.3 jit_solution(12413922294467366217)
XLA Ops:
  0.6 2.7 %outbox.1 = bf16[256,2688]{1,0:T(8,128)(2,1)} custom-call(s32[1,128]{1,0:T(1,128)} %bitcast.25, s32[1,128]{1,0:T(1,128)} %refs_1_.1, bf16[128,1024]{1,0:T(8,128)(2,1)} %bitcast.28, bf16[128,256]{1,0:T(8,128)(2,1)} %bitcast.23), custom_call_target="tpu_custom_call" | custom-call | flops 1 | bytes 1 | tf_op jit(solution)/shard_map/outbox/pallas_call | solution.py:91
  3.4 7.3 %all-to-all-start = ((bf16[8,32,2688]{2,1,0:T(8,128)(2,1)}), bf16[8,32,2688]{2,1,0:T(8,128)(2,1)S(1)}, u32[]{:S(2)}, u32[]{:S(2)}) async-start(bf16[8,32,2688]{2,1,0:T(8,128)(2,1)} %bitcast.27), calls=%async_computation | async-start | bytes 2752512 | tf_op jit(solution)/shard_map/all_to_all | solution.py:628
  10.7 1.3 slice_bitcast_fusion.2
  11.9 4.0 %collective-permute-start = (bf16[4,256,256]{2,1,0:T(8,128)(2,1)S(1)}, bf16[4,256,256]{2,1,0:T(8,128)(2,1)S(1)}, u32[]{:S(2)}, u32[]{:S(2)}) collective-permute-start(bf16[4,256,256]{2,1,0:T(8,128)(2,1)S(1)} %get-tuple-element.45), channel_id=1, source_target_pairs={{0,4},{4,8},{8,12},{12,16},{16,20},{20,24},{24,28},{1,5},{5,9},{9,... | collective-permute-start | bytes 1572872 | tf_op jit(solution)/shard_map/ppermute | solution.py:631
  15.9 1.3 collective-permute-start.1
  17.2 3.1 %slice_bitcast_fusion = (bf16[8,256,256]{2,1,0:T(8,128)(2,1)}, bf16[8,256,256]{2,1,0:T(8,128)(2,1)}) fusion(bf16[1,32,256,256]{3,2,1,0:T(8,128)(2,1)} %movie.1), kind=kLoop, calls=%fused_computation | loop fusion | bytes 4194304 | tf_op jit(solution)/shard_map/squeeze | solution.py:635
  20.3 27.8 %collective-permute-done.movie_prev = bf16[4,256,256]{2,1,0:T(8,128)(2,1)S(1)} collective-permute-done((bf16[4,256,256]{2,1,0:T(8,128)(2,1)S(1)}, bf16[4,256,256]{2,1,0:T(8,128)(2,1)S(1)}, u32[]{:S(2)}, u32[]{:S(2)}) %collective-permute-start) | collective-permute-done | bytes 524320 | tf_op jit(solution)/shard_map/ppermute | solution.py:631
  48.0 0.0 copy-start
  48.0 0.8 copy-done
  48.8 0.0 collective-permute-done.1.movie_next
  48.8 0.0 copy-start.2
  48.9 0.8 copy-done.2
  49.6 4.4 %collective-permute-start.2 = (bf16[8,256,256]{2,1,0:T(8,128)(2,1)}, bf16[8,256,256]{2,1,0:T(8,128)(2,1)S(1)}, u32[]{:S(2)}, u32[]{:S(2)}) collective-permute-start(bf16[8,256,256]{2,1,0:T(8,128)(2,1)} %get-tuple-element.26), channel_id=1, source_target_pairs={{0,4},{4,8},{8,12},{12,16},{16,20},{20,24},{24,28},{1,5},{5,9},{9,... | collective-permute-start | bytes 3145736 | tf_op jit(solution)/shard_map/ppermute | solution.py:631
  54.1 1.3 collective-permute-start.3
  55.4 0.0 all-to-all-done
  55.4 0.0 copy-start.1
  55.4 0.0 copy-start.3
  55.4 11.9 %residual.1 = (bf16[32,256,256]{2,1,0:T(8,128)(2,1)S(1)}, bf16[32,256,256]{2,1,0:T(8,128)(2,1)S(1)}, f32[8,4,256]{2,1,0:T(4,128)S(1)}) custom-call(bf16[256,2688]{1,0:T(8,128)(2,1)S(1)} %bitcast.19, bf16[1,32,256,256]{3,2,1,0:T(8,128)(2,1)} %movie.1), custom_call_target="tpu_custom_call" | custom-call | flops 1 | bytes 1 | tf_op jit(solution)/shard_map/residual/pallas_call | solution.py:212
  67.3 0.0 copy-done.1
  67.3 0.0 copy-done.3
  67.3 1.9 %near.1 = (bf16[8,256,256]{2,1,0:T(8,128)(2,1)S(1)}, bf16[8,256,256]{2,1,0:T(8,128)(2,1)S(1)}, f32[40,256]{1,0:T(8,128)S(1)}) custom-call(bf16[256,2688]{1,0:T(8,128)(2,1)S(1)} %bitcast.20, bf16[4,256,256]{2,1,0:T(8,128)(2,1)S(1)} %copy-done.3, bf16[4,256,256]{2,1,0:T(8,128)(2,1)S(1)} %copy-done.1, f32[8,4,256]{2,1,0:T(4,128)S(1)} %get-tuple-element.31.own_noise), custom_call_target="tpu_custom_call" | custom-call | flops 1 | bytes 1 | tf_op jit(solution)/shard_map/near/pallas_call | solution.py:257
  69.2 0.0 copy-start.5
  69.2 1.3 collective-permute-start.4
  70.5 1.5 %collective-permute-start.5 = (f32[40,256]{1,0:T(8,128)S(1)}, f32[40,256]{1,0:T(8,128)S(1)}, u32[]{:S(2)}, u32[]{:S(2)}) collective-permute-start(f32[40,256]{1,0:T(8,128)S(1)} %get-tuple-element.33.noise), channel_id=1, source_target_pairs={{1,0},{2,1},{3,2},{5,4},{6,5},{7,6},{9,8},{10,9},{11,10},{13,12},{... | collective-permute-start | bytes 122888 | tf_op jit(solution)/shard_map/ppermute | solution.py:645
  72.0 2.7 %outer_model.1.model = f32[16,256,256]{2,1,0:T(8,128)S(1)} custom-call(bf16[256,2688]{1,0:T(8,128)(2,1)S(1)} %bitcast.21), custom_call_target="tpu_custom_call" | custom-call | flops 1 | bytes 1 | tf_op jit(solution)/shard_map/outer_model/pallas_call | solution.py:282
  74.7 0.0 collective-permute-done.4.noise_before
  74.7 0.6 collective-permute-done.5.noise_after
  75.3 5.2 %weights.1 = (bf16[32,256,256]{2,1,0:T(8,128)(2,1)S(1)}, bf16[3,256,256]{2,1,0:T(8,128)(2,1)S(1)}, bf16[3,256,256]{2,1,0:T(8,128)(2,1)S(1)}) custom-call(bf16[32,256,256]{2,1,0:T(8,128)(2,1)S(1)} %get-tuple-element.28.own, bf16[8,256,256]{2,1,0:T(8,128)(2,1)S(1)} %get-tuple-element.32.near, f32[40,256]{1,0:T(8,128)S(1)} %get-tuple-element.33.noise, ...), custom_call_target="tpu_custom_call" | custom-call | flops 1 | bytes 1 | tf_op jit(solution)/shard_map/weights/pallas_call | solution.py:356
  80.6 0.0 copy-done.5
  80.6 3.9 %annulus_middle.1 = (bf16[1,32,256,256]{3,2,1,0:T(8,128)(2,1)}, f32[256,256]{1,0:T(8,128)S(1)}, f32[256,256]{1,0:T(8,128)S(1)}, f32[256,256]{1,0:T(8,128)S(1)}) custom-call(bf16[32,256,256]{2,1,0:T(8,128)(2,1)S(1)} %get-tuple-element.24.own, bf16[8,256,256]{2,1,0:T(8,128)(2,1)S(1)} %get-tuple-element.37.near, ...), custom_call_target="tpu_custom_call" | custom-call | flops 1 | bytes 1 | tf_op jit(solution)/shard_map/annulus_middle/pallas_call | solution.py:524
  84.5 13.9 %collective-permute-done.2.movie_prev = bf16[8,256,256]{2,1,0:T(8,128)(2,1)S(1)} collective-permute-done((bf16[8,256,256]{2,1,0:T(8,128)(2,1)}, bf16[8,256,256]{2,1,0:T(8,128)(2,1)S(1)}, u32[]{:S(2)}, u32[]{:S(2)}) %collective-permute-start.2) | collective-permute-done | bytes 1048608 | tf_op jit(solution)/shard_map/ppermute | solution.py:631
  98.3 0.0 collective-permute-done.3.movie_next
  98.3 0.0 copy-start.9
  98.3 0.0 copy-start.4
  98.3 0.0 copy-start.6
  98.4 0.0 copy-start.7
  98.4 0.0 copy-start.8
  98.4 4.7 %annulus_ends.1 = (bf16[1,32,256,256]{3,2,1,0:T(8,128)(2,1)}, bf16[256,1024]{1,0:T(8,128)(2,1)}) custom-call(bf16[32,256,256]{2,1,0:T(8,128)(2,1)S(1)} %get-tuple-element.24.own, bf16[8,256,256]{2,1,0:T(8,128)(2,1)S(1)} %collective-permute-done.2.movie_prev, ...), custom_call_target="tpu_custom_call", output_to_operand_aliasing={{0}: (8, {})} | custom-call | flops 1 | bytes 1 | tf_op jit(solution)/shard_map/annulus_ends/pallas_call | solution.py:524
  103.1 11.4 %all-to-all-start.1 = ((bf16[8,32,1024]{2,1,0:T(8,128)(2,1)}), bf16[8,32,1024]{2,1,0:T(8,128)(2,1)S(1)}, u32[]{:S(2)}, u32[]{:S(2)}) async-start(bf16[8,32,1024]{2,1,0:T(8,128)(2,1)} %bitcast.10), calls=%async_computation.1 | async-start | bytes 1048576 | tf_op jit(solution)/shard_map/all_to_all | solution.py:652
  114.4 0.0 copy-done.9
  114.4 0.1 multiply_reduce_fusion
  114.6 14.5 %all-to-all-done.1 = bf16[8,32,1024]{2,1,0:T(8,128)(2,1)S(1)} async-done(((bf16[8,32,1024]{2,1,0:T(8,128)(2,1)}), bf16[8,32,1024]{2,1,0:T(8,128)(2,1)S(1)}, u32[]{:S(2)}, u32[]{:S(2)}) %all-to-all-start.1) | async-done | bytes 524320 | tf_op jit(solution)/shard_map/all_to_all | solution.py:652
  129.1 0.0 copy-done.4
  129.1 0.0 copy-done.6
  129.1 0.0 copy-done.7
  129.1 0.0 copy-done.8
  129.1 2.2 %traces.1 = f32[128,256]{1,0:T(8,128)} custom-call(s32[1,128]{1,0:T(1,128)S(1)} %bitcast.26, f32[1,128]{1,0:T(1,128)S(1)} %copy-done.7, f32[1,128]{1,0:T(1,128)S(1)} %copy-done.8, f32[1,128]{1,0:T(1,128)S(1)} %divide_bitcast_fusion.step, bf16[128,256]{1,0:T(8,128)(2,1)S(1)} %bitcast.24, bf16[256,1024]{1,0:T(8,128)(2,1)S(1)} %bitcast.22), custom_call_target="tpu_custom_call" | custom-call | flops 1 | bytes 1 | tf_op jit(solution)/shard_map/traces/pallas_call | solution.py:601
  (1 shorter events, 0.0 us)
Async XLA Ops:
  3.4 52.0 %all-to-all-start = ((bf16[8,32,2688]{2,1,0:T(8,128)(2,1)}), bf16[8,32,2688]{2,1,0:T(8,128)(2,1)S(1)}, u32[]{:S(2)}, u32[]{:S(2)}) async-start(bf16[8,32,2688]{2,1,0:T(8,128)(2,1)} %bitcast.27), calls=%async_computation | async-start | bytes 2752512 | tf_op jit(solution)/shard_map/all_to_all | solution.py:628
  11.9 36.1 %collective-permute-start = (bf16[4,256,256]{2,1,0:T(8,128)(2,1)S(1)}, bf16[4,256,256]{2,1,0:T(8,128)(2,1)S(1)}, u32[]{:S(2)}, u32[]{:S(2)}) collective-permute-start(bf16[4,256,256]{2,1,0:T(8,128)(2,1)S(1)} %get-tuple-element.45), channel_id=1, source_target_pairs={{0,4},{4,8},{8,12},{12,16},{16,20},{20,24},{24,28},{1,5},{5,9},{9,... | collective-permute-start | bytes 1572872 | tf_op jit(solution)/shard_map/ppermute | solution.py:631
  15.9 32.9 %collective-permute-start.1 = (bf16[4,256,256]{2,1,0:T(8,128)(2,1)S(1)}, bf16[4,256,256]{2,1,0:T(8,128)(2,1)S(1)}, u32[]{:S(2)}, u32[]{:S(2)}) collective-permute-start(bf16[4,256,256]{2,1,0:T(8,128)(2,1)S(1)} %get-tuple-element.44), channel_id=1, source_target_pairs={{4,0},{8,4},{12,8},{16,12},{20,16},{24,20},{28,24},{5,1},{9,5},{13... | collective-permute-start | bytes 1572872 | tf_op jit(solution)/shard_map/ppermute | solution.py:631
  48.0 0.8 copy-start
  48.8 0.8 copy-start.2
  49.6 48.7 %collective-permute-start.2 = (bf16[8,256,256]{2,1,0:T(8,128)(2,1)}, bf16[8,256,256]{2,1,0:T(8,128)(2,1)S(1)}, u32[]{:S(2)}, u32[]{:S(2)}) collective-permute-start(bf16[8,256,256]{2,1,0:T(8,128)(2,1)} %get-tuple-element.26), channel_id=1, source_target_pairs={{0,4},{4,8},{8,12},{12,16},{16,20},{20,24},{24,28},{1,5},{5,9},{9,... | collective-permute-start | bytes 3145736 | tf_op jit(solution)/shard_map/ppermute | solution.py:631
  54.1 44.2 %collective-permute-start.3 = (bf16[8,256,256]{2,1,0:T(8,128)(2,1)}, bf16[8,256,256]{2,1,0:T(8,128)(2,1)S(1)}, u32[]{:S(2)}, u32[]{:S(2)}) collective-permute-start(bf16[8,256,256]{2,1,0:T(8,128)(2,1)} %get-tuple-element.27), channel_id=1, source_target_pairs={{4,0},{8,4},{12,8},{16,12},{20,16},{24,20},{28,24},{5,1},{9,5},{13... | collective-permute-start | bytes 3145736 | tf_op jit(solution)/shard_map/ppermute | solution.py:631
  55.4 11.9 %copy-start.1 = (bf16[4,256,256]{2,1,0:T(8,128)(2,1)S(1)}, bf16[4,256,256]{2,1,0:T(8,128)(2,1)}, u32[]{:S(2)}) copy-start(bf16[4,256,256]{2,1,0:T(8,128)(2,1)} %copy-done) | copy-start | bytes 1572868
  55.4 11.9 %copy-start.3 = (bf16[4,256,256]{2,1,0:T(8,128)(2,1)S(1)}, bf16[4,256,256]{2,1,0:T(8,128)(2,1)}, u32[]{:S(2)}) copy-start(bf16[4,256,256]{2,1,0:T(8,128)(2,1)} %copy-done.2) | copy-start | bytes 1572868
  69.2 11.4 %copy-start.5 = (f32[1,256]{1,0:T(1,128)S(1)}, f32[1,256]{1,0:T(1,128)}, u32[]{:S(2)}) copy-start(f32[1,256]{1,0:T(1,128)} %gain.3) | copy-start | bytes 3076
  69.2 5.5 %collective-permute-start.4 = (f32[40,256]{1,0:T(8,128)S(1)}, f32[40,256]{1,0:T(8,128)S(1)}, u32[]{:S(2)}, u32[]{:S(2)}) collective-permute-start(f32[40,256]{1,0:T(8,128)S(1)} %get-tuple-element.33.noise), channel_id=1, source_target_pairs={{0,1},{1,2},{2,3},{4,5},{5,6},{6,7},{8,9},{9,10},{10,11},{12,13},{... | collective-permute-start | bytes 122888 | tf_op jit(solution)/shard_map/ppermute | solution.py:644
  70.5 4.8 %collective-permute-start.5 = (f32[40,256]{1,0:T(8,128)S(1)}, f32[40,256]{1,0:T(8,128)S(1)}, u32[]{:S(2)}, u32[]{:S(2)}) collective-permute-start(f32[40,256]{1,0:T(8,128)S(1)} %get-tuple-element.33.noise), channel_id=1, source_target_pairs={{1,0},{2,1},{3,2},{5,4},{6,5},{7,6},{9,8},{10,9},{11,10},{13,12},{... | collective-permute-start | bytes 122888 | tf_op jit(solution)/shard_map/ppermute | solution.py:645
  98.3 16.1 %copy-start.9 = (bf16[1,128,1024]{2,1,0:T(8,128)(2,1)S(1)}, bf16[1,128,1024]{2,1,0:T(8,128)(2,1)}, u32[]{:S(2)}) copy-start(bf16[1,128,1024]{2,1,0:T(8,128)(2,1)} %param.9) | copy-start | bytes 786436
  98.3 30.7 %copy-start.4 = (bf16[1,128,256]{2,1,0:T(8,128)(2,1)S(1)}, bf16[1,128,256]{2,1,0:T(8,128)(2,1)}, u32[]{:S(2)}) copy-start(bf16[1,128,256]{2,1,0:T(8,128)(2,1)} %param.10) | copy-start | bytes 196612
  98.3 30.7 %copy-start.6 = (s32[1,128,1]{1,2,0:T(1,128)S(1)}, s32[1,128,1]{1,2,0:T(1,128)}, u32[]{:S(2)}) copy-start(s32[1,128,1]{1,2,0:T(1,128)} %param.11) | copy-start | bytes 1540
  98.4 30.7 %copy-start.7 = (f32[1,128]{1,0:T(1,128)S(1)}, f32[1,128]{1,0:T(1,128)}, u32[]{:S(2)}) copy-start(f32[1,128]{1,0:T(1,128)} %slow.1) | copy-start | bytes 1540
  98.4 30.7 %copy-start.8 = (f32[1,128]{1,0:T(1,128)S(1)}, f32[1,128]{1,0:T(1,128)}, u32[]{:S(2)}) copy-start(f32[1,128]{1,0:T(1,128)} %fast.1) | copy-start | bytes 1540
  103.1 26.0 %all-to-all-start.1 = ((bf16[8,32,1024]{2,1,0:T(8,128)(2,1)}), bf16[8,32,1024]{2,1,0:T(8,128)(2,1)S(1)}, u32[]{:S(2)}, u32[]{:S(2)}) async-start(bf16[8,32,1024]{2,1,0:T(8,128)(2,1)} %bitcast.10), calls=%async_computation.1 | async-start | bytes 1048576 | tf_op jit(solution)/shard_map/all_to_all | solution.py:652

commit v2 on v1

--- a/solution.py
+++ b/solution.py
@@ -43,6 +43,34 @@
 
 def dot(a, b):
     return jnp.dot(a, b, preferred_element_type=F32)
+
+
+def cut_kernel(movie, near_prev, near_next, up, down, sems):
+    del near_prev, near_next
+    rows, count = movie.shape[1], up.shape[0]
+    copies = [
+        pltpu.make_async_copy(movie.at[0, pl.ds(first, count)], out, sems.at[k])
+        for k, (first, out) in enumerate(((rows - NEAR - count, up), (NEAR, down)))
+    ]
+    for copy in copies:
+        copy.start()
+    for copy in copies:
+        copy.wait()
+
+
+def cut_outer(movie, near_prev, near_next):
+    cols, frames = movie.shape[2:]
+    piece = jax.ShapeDtypeStruct((RAD - NEAR, cols, frames), BF16)
+    return pl.pallas_call(
+        cut_kernel,
+        in_specs=[HBM, HBM, HBM],
+        out_specs=[VMEM, VMEM],
+        out_shape=(piece, piece),
+        scratch_shapes=[pltpu.SemaphoreType.DMA((2,))],
+        compiler_params=params(),
+        cost_estimate=pl.CostEstimate(flops=9 * 10**9, bytes_accessed=1, transcendentals=0),
+        name="cut_outer",
+    )(movie, near_prev, near_next)
 
 
 def outbox_kernel(capacity, *refs):
@@ -624,18 +652,12 @@
 
     stripe_row = stripe.reshape(1, count)
     outbox = make_outbox(stripe_row, column, footprints[0], traces[0], capacity, slots)
-    frames_in, outbox = lax.optimization_barrier((movie, outbox))
-    inbox = lax.all_to_all(outbox, "pix", split_axis=0, concat_axis=0, tiled=True)
-
     def exchange(cut):
         return (lax.ppermute(cut[0], "pix", pix_up), lax.ppermute(cut[1], "pix", pix_down))
 
-    near = exchange((frames_in[0, rows - NEAR :], frames_in[0, :NEAR]))
-    cut, near = lax.optimization_barrier(
-        ((frames_in[0, rows - RAD : rows - NEAR], frames_in[0, NEAR:RAD]), near)
-    )
-    outer_prev, outer_next = exchange(cut)
-    near_prev, near_next = near
+    near_prev, near_next = exchange((movie[0, rows - NEAR :], movie[0, :NEAR]))
+    outer_prev, outer_next = exchange(cut_outer(movie, near_prev, near_next))
+    inbox = lax.all_to_all(outbox, "pix", split_axis=0, concat_axis=0, tiled=True)
 
     foot_rows, residual, noise = make_residual(inbox, movie)
     near_rows, near_residual, noise = make_near(inbox, near_next, near_prev, noise)

time: 132 us -> 134 us (1.015)
  waiting for transfers between devices: 56.8 us -> 59.9 us
  local copies, waits for them, and re-layouts: 5.97 us -> 3.69 us
  Pallas kernels: 35.2 us -> 36.7 us
    ppermute x2, waiting for transfers between devices: 41.6 us -> 44.7 us  [exchange(): lax.ppermute(cut[0], 'pix', pix_up)]
    squeeze x2 -> x1, local copies, waits for them, and re-layouts: 4.34 us -> 1.27 us  [on_device(): near_prev, near_next = exchange((movie[0, rows - NEAR:], movie[0, :NEAR]))]
    pallas_call x0 -> x1, Pallas kernels: none -> 1.53 us  [cut_outer(): pl.pallas_call(cut_kernel, in_specs=[HBM, HBM, HBM], out_specs=[VMEM, VME...]
  transfers between devices with their start and end apart: 8 -> 8, of which waited for: 4 -> 4; matrix products, arithmetic and copies ran while one was open for 3% -> 1% of each run, Pallas kernels for 19% -> 20%
where the time goes in v2:
time: 134 us
  waiting for transfers between devices  59.9 us (45%)
  Pallas kernels  36.7 us (27%)
  starting transfers between devices  32.4 us (24%)
  local copies, waits for them, and re-layouts  3.69 us (3%)
    ppermute x2, waiting for transfers between devices, exchange(): lax.ppermute(cut[0], 'pix', pix_up)  44.7 us
    all_to_all x1, waiting for transfers between devices, on_device(): lax.all_to_all(gradient, 'pix', split_axis=0, concat_axis=0, tiled=True)  14.5 us
    pallas_call x1, Pallas kernels, make_residual(): pl.pallas_call(residual_kernel, in_specs=[VMEM, HBM], out_specs=[HBM, HBM...  11.9 us
    all_to_all x1, starting transfers between devices, on_device(): lax.all_to_all(gradient, 'pix', split_axis=0, concat_axis=0, tiled=True)  11.4 us
    pallas_call x2, Pallas kernels, call(): pl.pallas_call(kernel, in_specs=specs, out_specs=[HBM] + [VMEM] * (len(ou...  8.52 us
    ppermute x2, starting transfers between devices, exchange(): lax.ppermute(cut[0], 'pix', pix_up)  8.41 us
    all_to_all x1, starting transfers between devices, on_device(): lax.all_to_all(outbox, 'pix', split_axis=0, concat_axis=0, tiled=True)  7.29 us
    pallas_call x1, Pallas kernels, make_weights(): pl.pallas_call(functools.partial(weights_kernel, [float(t) for t in tap_v...  5.23 us
  transfers between devices with their start and end apart: 8, of which 4 were waited for; matrix products, arithmetic and copies ran while one was open for 1% of the time, Pallas kernels for 20%

profile of v2, /device:TPU:0, one launch (start us, length us, event | category | flops | bytes accessed | tf_op | source)
XLA Modules:
  0.0 133.7 jit_solution(847915532888655462)
XLA Ops:
  0.6 2.7 %outbox.1 = bf16[256,2688]{1,0:T(8,128)(2,1)} custom-call(s32[1,128]{1,0:T(1,128)} %bitcast.21, s32[1,128]{1,0:T(1,128)} %refs_1_.1, bf16[128,1024]{1,0:T(8,128)(2,1)} %bitcast.24, bf16[128,256]{1,0:T(8,128)(2,1)} %bitcast.19), custom_call_target="tpu_custom_call" | custom-call | flops 1 | bytes 1 | tf_op jit(solution)/shard_map/outbox/pallas_call | solution.py:119
  3.4 7.3 %all-to-all-start = ((bf16[8,32,2688]{2,1,0:T(8,128)(2,1)}), bf16[8,32,2688]{2,1,0:T(8,128)(2,1)S(1)}, u32[]{:S(2)}, u32[]{:S(2)}) async-start(bf16[8,32,2688]{2,1,0:T(8,128)(2,1)} %bitcast.23), calls=%async_computation | async-start | bytes 2752512 | tf_op jit(solution)/shard_map/all_to_all | solution.py:660
  10.7 1.3 slice_bitcast_fusion
  11.9 4.0 %collective-permute-start = (bf16[4,256,256]{2,1,0:T(8,128)(2,1)S(1)}, bf16[4,256,256]{2,1,0:T(8,128)(2,1)S(1)}, u32[]{:S(2)}, u32[]{:S(2)}) collective-permute-start(bf16[4,256,256]{2,1,0:T(8,128)(2,1)S(1)} %get-tuple-element.37), channel_id=1, source_target_pairs={{0,4},{4,8},{8,12},{12,16},{16,20},{20,24},{24,28},{1,5},{5,9},{9,... | collective-permute-start | bytes 1572872 | tf_op jit(solution)/shard_map/ppermute | solution.py:656
  15.9 1.3 collective-permute-start.1
  17.2 30.8 %collective-permute-done.near_prev.movie_prev = bf16[4,256,256]{2,1,0:T(8,128)(2,1)S(1)} collective-permute-done((bf16[4,256,256]{2,1,0:T(8,128)(2,1)S(1)}, bf16[4,256,256]{2,1,0:T(8,128)(2,1)S(1)}, u32[]{:S(2)}, u32[]{:S(2)}) %collective-permute-start) | collective-permute-done | bytes 524320 | tf_op jit(solution)/shard_map/ppermute | solution.py:656
  48.0 0.0 copy-start.1
  48.0 0.0 collective-permute-done.1.near_next.movie_next
  48.1 0.0 copy-start
  48.1 2.4 %copy-done = bf16[1,32,256,256]{3,2,1,0:T(8,128)(2,1)S(1)} copy-done((bf16[1,32,256,256]{3,2,1,0:T(8,128)(2,1)S(1)}, bf16[1,32,256,256]{3,2,1,0:T(8,128)(2,1)}, u32[]{:S(2)}) %copy-start) | copy-done | bytes 4194328
  50.4 0.0 copy-start.3
  50.4 1.5 %cut_outer.1 = (bf16[8,256,256]{2,1,0:T(8,128)(2,1)}, bf16[8,256,256]{2,1,0:T(8,128)(2,1)}) custom-call(bf16[1,32,256,256]{3,2,1,0:T(8,128)(2,1)S(1)} %copy-done, bf16[4,256,256]{2,1,0:T(8,128)(2,1)S(1)} %collective-permute-done.near_prev.movie_prev, bf16[4,256,256]{2,1,0:T(8,128)(2,1)S(1)} %collective-permute-done.1.near_next.movie_next), custom_call_target="tpu_custom_call" | custom-call | flops 8999999488 | bytes 1 | tf_op jit(solution)/shard_map/cut_outer/pallas_call | solution.py:64
  52.0 0.0 copy-done.1
  52.0 0.0 copy-done.3
  52.0 4.5 %collective-permute-start.2 = (bf16[8,256,256]{2,1,0:T(8,128)(2,1)}, bf16[8,256,256]{2,1,0:T(8,128)(2,1)S(1)}, u32[]{:S(2)}, u32[]{:S(2)}) collective-permute-start(bf16[8,256,256]{2,1,0:T(8,128)(2,1)} %get-tuple-element.20), channel_id=1, source_target_pairs={{0,4},{4,8},{8,12},{12,16},{16,20},{20,24},{24,28},{1,5},{5,9},{9,... | collective-permute-start | bytes 3145736 | tf_op jit(solution)/shard_map/ppermute | solution.py:656
  56.4 1.3 collective-permute-start.3
  57.7 0.0 all-to-all-done
  57.8 0.0 copy-start.2
  57.8 0.0 copy-start.4
  57.8 11.9 %residual.1 = (bf16[32,256,256]{2,1,0:T(8,128)(2,1)S(1)}, bf16[32,256,256]{2,1,0:T(8,128)(2,1)S(1)}, f32[8,4,256]{2,1,0:T(4,128)S(1)}) custom-call(bf16[256,2688]{1,0:T(8,128)(2,1)S(1)} %bitcast.15, bf16[1,32,256,256]{3,2,1,0:T(8,128)(2,1)} %movie.3), custom_call_target="tpu_custom_call" | custom-call | flops 1 | bytes 1 | tf_op jit(solution)/shard_map/residual/pallas_call | solution.py:240
  69.6 0.0 copy-done.2
  69.7 0.0 copy-done.4
  69.7 1.9 %near.1 = (bf16[8,256,256]{2,1,0:T(8,128)(2,1)S(1)}, bf16[8,256,256]{2,1,0:T(8,128)(2,1)S(1)}, f32[40,256]{1,0:T(8,128)S(1)}) custom-call(bf16[256,2688]{1,0:T(8,128)(2,1)S(1)} %bitcast.16, bf16[4,256,256]{2,1,0:T(8,128)(2,1)S(1)} %copy-done.4, bf16[4,256,256]{2,1,0:T(8,128)(2,1)S(1)} %copy-done.2, f32[8,4,256]{2,1,0:T(4,128)S(1)} %get-tuple-element.23.own_noise), custom_call_target="tpu_custom_call" | custom-call | flops 1 | bytes 1 | tf_op jit(solution)/shard_map/near/pallas_call | solution.py:285
  71.6 0.0 copy-start.6
  71.6 1.3 collective-permute-start.4
  72.9 1.5 %collective-permute-start.5 = (f32[40,256]{1,0:T(8,128)S(1)}, f32[40,256]{1,0:T(8,128)S(1)}, u32[]{:S(2)}, u32[]{:S(2)}) collective-permute-start(f32[40,256]{1,0:T(8,128)S(1)} %get-tuple-element.25.noise), channel_id=1, source_target_pairs={{1,0},{2,1},{3,2},{5,4},{6,5},{7,6},{9,8},{10,9},{11,10},{13,12},{... | collective-permute-start | bytes 122888 | tf_op jit(solution)/shard_map/ppermute | solution.py:667
  74.3 2.7 %outer_model.1.model = f32[16,256,256]{2,1,0:T(8,128)S(1)} custom-call(bf16[256,2688]{1,0:T(8,128)(2,1)S(1)} %bitcast.17), custom_call_target="tpu_custom_call" | custom-call | flops 1 | bytes 1 | tf_op jit(solution)/shard_map/outer_model/pallas_call | solution.py:310
  77.1 0.0 collective-permute-done.4.noise_before
  77.1 0.6 collective-permute-done.5.noise_after
  77.7 5.2 %weights.1 = (bf16[32,256,256]{2,1,0:T(8,128)(2,1)S(1)}, bf16[3,256,256]{2,1,0:T(8,128)(2,1)S(1)}, bf16[3,256,256]{2,1,0:T(8,128)(2,1)S(1)}) custom-call(bf16[32,256,256]{2,1,0:T(8,128)(2,1)S(1)} %get-tuple-element.22.own, bf16[8,256,256]{2,1,0:T(8,128)(2,1)S(1)} %get-tuple-element.24.near, f32[40,256]{1,0:T(8,128)S(1)} %get-tuple-element.25.noise, ...), custom_call_target="tpu_custom_call" | custom-call | flops 1 | bytes 1 | tf_op jit(solution)/shard_map/weights/pallas_call | solution.py:384
  82.9 0.0 copy-done.6
  82.9 3.9 %annulus_middle.1 = (bf16[1,32,256,256]{3,2,1,0:T(8,128)(2,1)}, f32[256,256]{1,0:T(8,128)S(1)}, f32[256,256]{1,0:T(8,128)S(1)}, f32[256,256]{1,0:T(8,128)S(1)}) custom-call(bf16[32,256,256]{2,1,0:T(8,128)(2,1)S(1)} %get-tuple-element.19.own, bf16[8,256,256]{2,1,0:T(8,128)(2,1)S(1)} %get-tuple-element.29.near, ...), custom_call_target="tpu_custom_call" | custom-call | flops 1 | bytes 1 | tf_op jit(solution)/shard_map/annulus_middle/pallas_call | solution.py:552
  86.8 13.9 %collective-permute-done.2.movie_prev = bf16[8,256,256]{2,1,0:T(8,128)(2,1)S(1)} collective-permute-done((bf16[8,256,256]{2,1,0:T(8,128)(2,1)}, bf16[8,256,256]{2,1,0:T(8,128)(2,1)S(1)}, u32[]{:S(2)}, u32[]{:S(2)}) %collective-permute-start.2) | collective-permute-done | bytes 1048608 | tf_op jit(solution)/shard_map/ppermute | solution.py:656
  100.7 0.0 collective-permute-done.3.movie_next
  100.7 0.0 copy-start.10
  100.7 0.0 copy-start.5
  100.7 0.0 copy-start.7
  100.7 0.0 copy-start.8
  100.7 0.0 copy-start.9
  100.7 4.7 %annulus_ends.1 = (bf16[1,32,256,256]{3,2,1,0:T(8,128)(2,1)}, bf16[256,1024]{1,0:T(8,128)(2,1)}) custom-call(bf16[32,256,256]{2,1,0:T(8,128)(2,1)S(1)} %get-tuple-element.19.own, bf16[8,256,256]{2,1,0:T(8,128)(2,1)S(1)} %collective-permute-done.2.movie_prev, ...), custom_call_target="tpu_custom_call", output_to_operand_aliasing={{0}: (8, {})} | custom-call | flops 1 | bytes 1 | tf_op jit(solution)/shard_map/annulus_ends/pallas_call | solution.py:552
  105.4 11.4 %all-to-all-start.1 = ((bf16[8,32,1024]{2,1,0:T(8,128)(2,1)}), bf16[8,32,1024]{2,1,0:T(8,128)(2,1)S(1)}, u32[]{:S(2)}, u32[]{:S(2)}) async-start(bf16[8,32,1024]{2,1,0:T(8,128)(2,1)} %bitcast.8), calls=%async_computation.1 | async-start | bytes 1048576 | tf_op jit(solution)/shard_map/all_to_all | solution.py:674
  116.8 0.0 copy-done.10
  116.8 0.1 multiply_reduce_fusion
  116.9 14.5 %all-to-all-done.1 = bf16[8,32,1024]{2,1,0:T(8,128)(2,1)S(1)} async-done(((bf16[8,32,1024]{2,1,0:T(8,128)(2,1)}), bf16[8,32,1024]{2,1,0:T(8,128)(2,1)S(1)}, u32[]{:S(2)}, u32[]{:S(2)}) %all-to-all-start.1) | async-done | bytes 524320 | tf_op jit(solution)/shard_map/all_to_all | solution.py:674
  131.4 0.0 copy-done.5
  131.4 0.0 copy-done.7
  131.4 0.0 copy-done.8
  131.4 0.0 copy-done.9
  131.5 2.2 %traces.1 = f32[128,256]{1,0:T(8,128)} custom-call(s32[1,128]{1,0:T(1,128)S(1)} %bitcast.22, f32[1,128]{1,0:T(1,128)S(1)} %copy-done.8, f32[1,128]{1,0:T(1,128)S(1)} %copy-done.9, f32[1,128]{1,0:T(1,128)S(1)} %divide_bitcast_fusion.step, bf16[128,256]{1,0:T(8,128)(2,1)S(1)} %bitcast.20, bf16[256,1024]{1,0:T(8,128)(2,1)S(1)} %bitcast.18), custom_call_target="tpu_custom_call" | custom-call | flops 1 | bytes 1 | tf_op jit(solution)/shard_map/traces/pallas_call | solution.py:629
  (1 shorter events, 0.0 us)
Async XLA Ops:
  3.4 54.4 %all-to-all-start = ((bf16[8,32,2688]{2,1,0:T(8,128)(2,1)}), bf16[8,32,2688]{2,1,0:T(8,128)(2,1)S(1)}, u32[]{:S(2)}, u32[]{:S(2)}) async-start(bf16[8,32,2688]{2,1,0:T(8,128)(2,1)} %bitcast.23), calls=%async_computation | async-start | bytes 2752512 | tf_op jit(solution)/shard_map/all_to_all | solution.py:660
  11.9 36.1 %collective-permute-start = (bf16[4,256,256]{2,1,0:T(8,128)(2,1)S(1)}, bf16[4,256,256]{2,1,0:T(8,128)(2,1)S(1)}, u32[]{:S(2)}, u32[]{:S(2)}) collective-permute-start(bf16[4,256,256]{2,1,0:T(8,128)(2,1)S(1)} %get-tuple-element.37), channel_id=1, source_target_pairs={{0,4},{4,8},{8,12},{12,16},{16,20},{20,24},{24,28},{1,5},{5,9},{9,... | collective-permute-start | bytes 1572872 | tf_op jit(solution)/shard_map/ppermute | solution.py:656
  15.9 32.1 %collective-permute-start.1 = (bf16[4,256,256]{2,1,0:T(8,128)(2,1)S(1)}, bf16[4,256,256]{2,1,0:T(8,128)(2,1)S(1)}, u32[]{:S(2)}, u32[]{:S(2)}) collective-permute-start(bf16[4,256,256]{2,1,0:T(8,128)(2,1)S(1)} %get-tuple-element.36), channel_id=1, source_target_pairs={{4,0},{8,4},{12,8},{16,12},{20,16},{24,20},{28,24},{5,1},{9,5},{13... | collective-permute-start | bytes 1572872 | tf_op jit(solution)/shard_map/ppermute | solution.py:656
  48.0 3.9 %copy-start.1 = (bf16[4,256,256]{2,1,0:T(8,128)(2,1)}, bf16[4,256,256]{2,1,0:T(8,128)(2,1)S(1)}, u32[]{:S(2)}) copy-start(bf16[4,256,256]{2,1,0:T(8,128)(2,1)S(1)} %collective-permute-done.near_prev.movie_prev) | copy-start | bytes 1572868
  48.1 2.4 %copy-start = (bf16[1,32,256,256]{3,2,1,0:T(8,128)(2,1)S(1)}, bf16[1,32,256,256]{3,2,1,0:T(8,128)(2,1)}, u32[]{:S(2)}) copy-start(bf16[1,32,256,256]{3,2,1,0:T(8,128)(2,1)} %movie.3) | copy-start | bytes 12582916
  50.4 1.6 %copy-start.3 = (bf16[4,256,256]{2,1,0:T(8,128)(2,1)}, bf16[4,256,256]{2,1,0:T(8,128)(2,1)S(1)}, u32[]{:S(2)}) copy-start(bf16[4,256,256]{2,1,0:T(8,128)(2,1)S(1)} %collective-permute-done.1.near_next.movie_next) | copy-start | bytes 1572868
  52.0 48.7 %collective-permute-start.2 = (bf16[8,256,256]{2,1,0:T(8,128)(2,1)}, bf16[8,256,256]{2,1,0:T(8,128)(2,1)S(1)}, u32[]{:S(2)}, u32[]{:S(2)}) collective-permute-start(bf16[8,256,256]{2,1,0:T(8,128)(2,1)} %get-tuple-element.20), channel_id=1, source_target_pairs={{0,4},{4,8},{8,12},{12,16},{16,20},{20,24},{24,28},{1,5},{5,9},{9,... | collective-permute-start | bytes 3145736 | tf_op jit(solution)/shard_map/ppermute | solution.py:656
  56.4 44.2 %collective-permute-start.3 = (bf16[8,256,256]{2,1,0:T(8,128)(2,1)}, bf16[8,256,256]{2,1,0:T(8,128)(2,1)S(1)}, u32[]{:S(2)}, u32[]{:S(2)}) collective-permute-start(bf16[8,256,256]{2,1,0:T(8,128)(2,1)} %get-tuple-element.21), channel_id=1, source_target_pairs={{4,0},{8,4},{12,8},{16,12},{20,16},{24,20},{28,24},{5,1},{9,5},{13... | collective-permute-start | bytes 3145736 | tf_op jit(solution)/shard_map/ppermute | solution.py:656
  57.8 11.9 %copy-start.2 = (bf16[4,256,256]{2,1,0:T(8,128)(2,1)S(1)}, bf16[4,256,256]{2,1,0:T(8,128)(2,1)}, u32[]{:S(2)}) copy-start(bf16[4,256,256]{2,1,0:T(8,128)(2,1)} %copy-done.1) | copy-start | bytes 1572868
  57.8 11.9 %copy-start.4 = (bf16[4,256,256]{2,1,0:T(8,128)(2,1)S(1)}, bf16[4,256,256]{2,1,0:T(8,128)(2,1)}, u32[]{:S(2)}) copy-start(bf16[4,256,256]{2,1,0:T(8,128)(2,1)} %copy-done.3) | copy-start | bytes 1572868
  71.6 11.4 %copy-start.6 = (f32[1,256]{1,0:T(1,128)S(1)}, f32[1,256]{1,0:T(1,128)}, u32[]{:S(2)}) copy-start(f32[1,256]{1,0:T(1,128)} %gain.3) | copy-start | bytes 3076
  71.6 5.5 %collective-permute-start.4 = (f32[40,256]{1,0:T(8,128)S(1)}, f32[40,256]{1,0:T(8,128)S(1)}, u32[]{:S(2)}, u32[]{:S(2)}) collective-permute-start(f32[40,256]{1,0:T(8,128)S(1)} %get-tuple-element.25.noise), channel_id=1, source_target_pairs={{0,1},{1,2},{2,3},{4,5},{5,6},{6,7},{8,9},{9,10},{10,11},{12,13},{... | collective-permute-start | bytes 122888 | tf_op jit(solution)/shard_map/ppermute | solution.py:666
  72.9 4.8 %collective-permute-start.5 = (f32[40,256]{1,0:T(8,128)S(1)}, f32[40,256]{1,0:T(8,128)S(1)}, u32[]{:S(2)}, u32[]{:S(2)}) collective-permute-start(f32[40,256]{1,0:T(8,128)S(1)} %get-tuple-element.25.noise), channel_id=1, source_target_pairs={{1,0},{2,1},{3,2},{5,4},{6,5},{7,6},{9,8},{10,9},{11,10},{13,12},{... | collective-permute-start | bytes 122888 | tf_op jit(solution)/shard_map/ppermute | solution.py:667
  100.7 16.1 %copy-start.10 = (bf16[1,128,1024]{2,1,0:T(8,128)(2,1)S(1)}, bf16[1,128,1024]{2,1,0:T(8,128)(2,1)}, u32[]{:S(2)}) copy-start(bf16[1,128,1024]{2,1,0:T(8,128)(2,1)} %param.9) | copy-start | bytes 786436
  100.7 30.7 %copy-start.5 = (bf16[1,128,256]{2,1,0:T(8,128)(2,1)S(1)}, bf16[1,128,256]{2,1,0:T(8,128)(2,1)}, u32[]{:S(2)}) copy-start(bf16[1,128,256]{2,1,0:T(8,128)(2,1)} %param.10) | copy-start | bytes 196612
  100.7 30.7 %copy-start.7 = (s32[1,128,1]{1,2,0:T(1,128)S(1)}, s32[1,128,1]{1,2,0:T(1,128)}, u32[]{:S(2)}) copy-start(s32[1,128,1]{1,2,0:T(1,128)} %param.11) | copy-start | bytes 1540
  100.7 30.7 %copy-start.8 = (f32[1,128]{1,0:T(1,128)S(1)}, f32[1,128]{1,0:T(1,128)}, u32[]{:S(2)}) copy-start(f32[1,128]{1,0:T(1,128)} %slow.1) | copy-start | bytes 1540
  100.7 30.7 %copy-start.9 = (f32[1,128]{1,0:T(1,128)S(1)}, f32[1,128]{1,0:T(1,128)}, u32[]{:S(2)}) copy-start(f32[1,128]{1,0:T(1,128)} %fast.1) | copy-start | bytes 1540
  105.4 26.0 %all-to-all-start.1 = ((bf16[8,32,1024]{2,1,0:T(8,128)(2,1)}), bf16[8,32,1024]{2,1,0:T(8,128)(2,1)S(1)}, u32[]{:S(2)}, u32[]{:S(2)}) async-start(bf16[8,32,1024]{2,1,0:T(8,128)(2,1)} %bitcast.8), calls=%async_computation.1 | async-start | bytes 1048576 | tf_op jit(solution)/shard_map/all_to_all | solution.py:674

commit v3 on v1

--- a/solution.py
+++ b/solution.py
@@ -586,14 +586,16 @@
 
     a, b = wide(slow), wide(fast)
     driven = updated - (a + b) * lagged(updated, 1) + (a * b) * lagged(updated, 2)
-    value = jnp.maximum(driven - lam_floor, 0.0) * ((1.0 - a) * (1.0 - b))
-    for root in (a, b):
-        lag = 1
-        while lag < frames:
-            value = value + root * lagged(value, lag)
-            root = root * root
-            lag *= 2
-    out[...] = value
+    spikes = jnp.maximum(driven - lam_floor, 0.0)
+    sums = [spikes, spikes]
+    roots = [a, b]
+    lag = 1
+    while lag < frames:
+        sums = [value + root * lagged(value, lag) for value, root in zip(sums, roots)]
+        roots = [root * root for root in roots]
+        lag *= 2
+    share = (1.0 - a) * (1.0 - b) / (a - b)
+    out[...] = share * (a * sums[0] - b * sums[1])
 
 
 def make_traces(stripe, slow, fast, step, traces, inbox, capacity):
@@ -630,12 +632,10 @@
     def exchange(cut):
         return (lax.ppermute(cut[0], "pix", pix_up), lax.ppermute(cut[1], "pix", pix_down))
 
-    near = exchange((frames_in[0, rows - NEAR :], frames_in[0, :NEAR]))
-    cut, near = lax.optimization_barrier(
-        ((frames_in[0, rows - RAD : rows - NEAR], frames_in[0, NEAR:RAD]), near)
-    )
-    outer_prev, outer_next = exchange(cut)
-    near_prev, near_next = near
+    near_prev, near_next = exchange((frames_in[0, rows - NEAR :], frames_in[0, :NEAR]))
+    outer_prev, outer_next = exchange(
+        (frames_in[0, rows - RAD : rows - NEAR], frames_in[0, NEAR:RAD])
+    )
 
     foot_rows, residual, noise = make_residual(inbox, movie)
     near_rows, near_residual, noise = make_near(inbox, near_next, near_prev, noise)

time: 132 us -> 143 us (1.083)
  waiting for transfers between devices: 56.8 us -> 67.7 us
    all_to_all x1, waiting for transfers between devices: 0.01 us -> 16.4 us  [on_device(): lax.all_to_all(outbox, 'pix', split_axis=0, concat_axis=0, tiled=True)]
    ppermute x2, waiting for transfers between devices: 41.6 us -> 30.6 us  [exchange(): lax.ppermute(cut[0], 'pix', pix_up)]
    ppermute x2, waiting for transfers between devices: 0.01 us -> 5.77 us  [exchange(): lax.ppermute(cut[1], 'pix', pix_down)]
    all_to_all x1, starting transfers between devices: 11.4 us -> 9.51 us  [on_device(): lax.all_to_all(gradient, 'pix', split_axis=0, concat_axis=0, tiled=True)]
    unnamed x20 -> x12, local copies, waits for them, and re-layouts: 1.63 us -> 0.04 us
    ppermute x2, starting transfers between devices: 8.4 us -> 9.95 us  [exchange(): lax.ppermute(cut[0], 'pix', pix_up)]
  transfers between devices with their start and end apart: 8 -> 8, of which waited for: 4 -> 5; matrix products, arithmetic and copies ran while one was open for 3% -> 4% of each run, Pallas kernels for 19% -> 19%
where the time goes in v3:
time: 143 us; the launch traced here: 142 us
  waiting for transfers between devices  67.7 us (47%)
  Pallas kernels  35.8 us (25%)
  starting transfers between devices  32.1 us (22%)
  local copies, waits for them, and re-layouts  5.35 us (4%)
    ppermute x2, waiting for transfers between devices, exchange(): lax.ppermute(cut[0], 'pix', pix_up)  30.6 us
    all_to_all x1, waiting for transfers between devices, on_device(): lax.all_to_all(outbox, 'pix', split_axis=0, concat_axis=0, tiled=True)  16.4 us
    all_to_all x1, waiting for transfers between devices, on_device(): lax.all_to_all(gradient, 'pix', split_axis=0, concat_axis=0, tiled=True)  14.3 us
    pallas_call x1, Pallas kernels, make_residual(): pl.pallas_call(residual_kernel, in_specs=[VMEM, HBM], out_specs=[HBM, HBM...  11.8 us
    ppermute x2, starting transfers between devices, exchange(): lax.ppermute(cut[0], 'pix', pix_up)  9.95 us
    all_to_all x1, starting transfers between devices, on_device(): lax.all_to_all(gradient, 'pix', split_axis=0, concat_axis=0, tiled=True)  9.51 us
    pallas_call x2, Pallas kernels, call(): pl.pallas_call(kernel, in_specs=specs, out_specs=[HBM] + [VMEM] * (len(ou...  8.52 us
    all_to_all x1, starting transfers between devices, on_device(): lax.all_to_all(outbox, 'pix', split_axis=0, concat_axis=0, tiled=True)  7.29 us
  transfers between devices with their start and end apart: 8, of which 5 were waited for; matrix products, arithmetic and copies ran while one was open for 4% of the time, Pallas kernels for 19%

profile of v3, /device:TPU:0, one launch (start us, length us, event | category | flops | bytes accessed | tf_op | source)
XLA Modules:
  0.0 141.8 jit_solution(18419319635549509373)
XLA Ops:
  0.6 2.7 %outbox.1 = bf16[256,2688]{1,0:T(8,128)(2,1)} custom-call(s32[1,128]{1,0:T(1,128)} %bitcast.25, s32[1,128]{1,0:T(1,128)} %refs_1_.1, bf16[128,1024]{1,0:T(8,128)(2,1)} %bitcast.28, bf16[128,256]{1,0:T(8,128)(2,1)} %bitcast.23), custom_call_target="tpu_custom_call" | custom-call | flops 1 | bytes 1 | tf_op jit(solution)/shard_map/outbox/pallas_call | solution.py:91
  3.4 7.3 %all-to-all-start = ((bf16[8,32,2688]{2,1,0:T(8,128)(2,1)}), bf16[8,32,2688]{2,1,0:T(8,128)(2,1)S(1)}, u32[]{:S(2)}, u32[]{:S(2)}) async-start(bf16[8,32,2688]{2,1,0:T(8,128)(2,1)} %bitcast.27), calls=%async_computation | async-start | bytes 2752512 | tf_op jit(solution)/shard_map/all_to_all | solution.py:630
  10.7 3.1 %slice_bitcast_fusion = (bf16[8,256,256]{2,1,0:T(8,128)(2,1)}, bf16[8,256,256]{2,1,0:T(8,128)(2,1)}) fusion(bf16[1,32,256,256]{3,2,1,0:T(8,128)(2,1)} %movie.1), kind=kLoop, calls=%fused_computation | loop fusion | bytes 4194304 | tf_op jit(solution)/shard_map/squeeze | solution.py:637
  13.7 4.0 %collective-permute-start = (bf16[8,256,256]{2,1,0:T(8,128)(2,1)}, bf16[8,256,256]{2,1,0:T(8,128)(2,1)S(1)}, u32[]{:S(2)}, u32[]{:S(2)}) collective-permute-start(bf16[8,256,256]{2,1,0:T(8,128)(2,1)} %get-tuple-element.39), channel_id=1, source_target_pairs={{0,4},{4,8},{8,12},{12,16},{16,20},{20,24},{24,28},{1,5},{5,9},{9,... | collective-permute-start | bytes 3145736 | tf_op jit(solution)/shard_map/ppermute | solution.py:633
  17.7 1.3 collective-permute-start.1
  19.0 2.3 %slice_bitcast_fusion.2 = (bf16[4,256,256]{2,1,0:T(8,128)(2,1)}, bf16[4,256,256]{2,1,0:T(8,128)(2,1)}) fusion(bf16[1,32,256,256]{3,2,1,0:T(8,128)(2,1)} %movie.1), kind=kLoop, calls=%fused_computation.3 | loop fusion | bytes 2097152 | tf_op jit(solution)/shard_map/squeeze | solution.py:635
  21.3 1.3 collective-permute-start.2
  22.6 6.0 %collective-permute-start.3 = (bf16[4,256,256]{2,1,0:T(8,128)(2,1)}, bf16[4,256,256]{2,1,0:T(8,128)(2,1)}, u32[]{:S(2)}, u32[]{:S(2)}) collective-permute-start(bf16[4,256,256]{2,1,0:T(8,128)(2,1)} %get-tuple-element.36), channel_id=1, source_target_pairs={{0,4},{4,8},{8,12},{12,16},{16,20},{20,24},{24,28},{1,5},{5,9},{9,... | collective-permute-start | bytes 1572872 | tf_op jit(solution)/shard_map/ppermute | solution.py:633
  28.5 16.4 %all-to-all-done = bf16[8,32,2688]{2,1,0:T(8,128)(2,1)S(1)} async-done(((bf16[8,32,2688]{2,1,0:T(8,128)(2,1)}), bf16[8,32,2688]{2,1,0:T(8,128)(2,1)S(1)}, u32[]{:S(2)}, u32[]{:S(2)}) %all-to-all-start) | async-done | bytes 1376288 | tf_op jit(solution)/shard_map/all_to_all | solution.py:630
  44.9 11.8 %residual.1 = (bf16[32,256,256]{2,1,0:T(8,128)(2,1)S(1)}, bf16[32,256,256]{2,1,0:T(8,128)(2,1)S(1)}, f32[8,4,256]{2,1,0:T(4,128)S(1)}) custom-call(bf16[256,2688]{1,0:T(8,128)(2,1)S(1)} %bitcast.19, bf16[1,32,256,256]{3,2,1,0:T(8,128)(2,1)} %movie.1), custom_call_target="tpu_custom_call" | custom-call | flops 1 | bytes 1 | tf_op jit(solution)/shard_map/residual/pallas_call | solution.py:212
  56.7 5.8 %collective-permute-done.2.movie_next = bf16[4,256,256]{2,1,0:T(8,128)(2,1)} collective-permute-done((bf16[4,256,256]{2,1,0:T(8,128)(2,1)}, bf16[4,256,256]{2,1,0:T(8,128)(2,1)}, u32[]{:S(2)}, u32[]{:S(2)}) %collective-permute-start.2) | collective-permute-done | bytes 524320 | tf_op jit(solution)/shard_map/ppermute | solution.py:633
  62.5 30.6 %collective-permute-done.3.movie_prev = bf16[4,256,256]{2,1,0:T(8,128)(2,1)} collective-permute-done((bf16[4,256,256]{2,1,0:T(8,128)(2,1)}, bf16[4,256,256]{2,1,0:T(8,128)(2,1)}, u32[]{:S(2)}, u32[]{:S(2)}) %collective-permute-start.3) | collective-permute-done | bytes 524320 | tf_op jit(solution)/shard_map/ppermute | solution.py:633
  93.1 3.1 %near.1 = (bf16[8,256,256]{2,1,0:T(8,128)(2,1)S(1)}, bf16[8,256,256]{2,1,0:T(8,128)(2,1)S(1)}, f32[40,256]{1,0:T(8,128)S(1)}) custom-call(bf16[256,2688]{1,0:T(8,128)(2,1)S(1)} %bitcast.20, bf16[4,256,256]{2,1,0:T(8,128)(2,1)} %collective-permute-done.2.movie_next, bf16[4,256,256]{2,1,0:T(8,128)(2,1)} %collective-permute-done.3.movie_prev, ...), custom_call_target="tpu_custom_call" | custom-call | flops 1 | bytes 1 | tf_op jit(solution)/shard_map/near/pallas_call | solution.py:257
  96.2 0.0 copy-start.1
  96.2 1.3 collective-permute-start.4
  97.5 1.5 %collective-permute-start.5 = (f32[40,256]{1,0:T(8,128)S(1)}, f32[40,256]{1,0:T(8,128)S(1)}, u32[]{:S(2)}, u32[]{:S(2)}) collective-permute-start(f32[40,256]{1,0:T(8,128)S(1)} %get-tuple-element.25.noise), channel_id=1, source_target_pairs={{1,0},{2,1},{3,2},{5,4},{6,5},{7,6},{9,8},{10,9},{11,10},{13,12},{... | collective-permute-start | bytes 122888 | tf_op jit(solution)/shard_map/ppermute | solution.py:645
  99.0 2.7 %outer_model.1.model = f32[16,256,256]{2,1,0:T(8,128)S(1)} custom-call(bf16[256,2688]{1,0:T(8,128)(2,1)S(1)} %bitcast.21), custom_call_target="tpu_custom_call" | custom-call | flops 1 | bytes 1 | tf_op jit(solution)/shard_map/outer_model/pallas_call | solution.py:282
  101.7 0.0 collective-permute-done.4.noise_before
  101.7 0.6 collective-permute-done.5.noise_after
  102.3 5.2 %weights.1 = (bf16[32,256,256]{2,1,0:T(8,128)(2,1)S(1)}, bf16[3,256,256]{2,1,0:T(8,128)(2,1)S(1)}, bf16[3,256,256]{2,1,0:T(8,128)(2,1)S(1)}) custom-call(bf16[32,256,256]{2,1,0:T(8,128)(2,1)S(1)} %get-tuple-element.22.own, bf16[8,256,256]{2,1,0:T(8,128)(2,1)S(1)} %get-tuple-element.24.near, f32[40,256]{1,0:T(8,128)S(1)} %get-tuple-element.25.noise, ...), custom_call_target="tpu_custom_call" | custom-call | flops 1 | bytes 1 | tf_op jit(solution)/shard_map/weights/pallas_call | solution.py:356
  107.6 0.0 copy-done.1
  107.6 3.9 %annulus_middle.1 = (bf16[1,32,256,256]{3,2,1,0:T(8,128)(2,1)}, f32[256,256]{1,0:T(8,128)S(1)}, f32[256,256]{1,0:T(8,128)S(1)}, f32[256,256]{1,0:T(8,128)S(1)}) custom-call(bf16[32,256,256]{2,1,0:T(8,128)(2,1)S(1)} %get-tuple-element.20.own, bf16[8,256,256]{2,1,0:T(8,128)(2,1)S(1)} %get-tuple-element.29.near, ...), custom_call_target="tpu_custom_call" | custom-call | flops 1 | bytes 1 | tf_op jit(solution)/shard_map/annulus_middle/pallas_call | solution.py:524
  111.4 0.0 collective-permute-done.movie_prev
  111.5 0.0 collective-permute-done.1.movie_next
  111.5 0.0 copy-start.5
  111.5 0.0 copy-start
  111.5 0.0 copy-start.2
  111.5 0.0 copy-start.3
  111.5 0.0 copy-start.4
  111.5 4.7 %annulus_ends.1 = (bf16[1,32,256,256]{3,2,1,0:T(8,128)(2,1)}, bf16[256,1024]{1,0:T(8,128)(2,1)}) custom-call(bf16[32,256,256]{2,1,0:T(8,128)(2,1)S(1)} %get-tuple-element.20.own, bf16[8,256,256]{2,1,0:T(8,128)(2,1)S(1)} %collective-permute-done.movie_prev, ...), custom_call_target="tpu_custom_call", output_to_operand_aliasing={{0}: (8, {})} | custom-call | flops 1 | bytes 1 | tf_op jit(solution)/shard_map/annulus_ends/pallas_call | solution.py:524
  116.2 9.5 %all-to-all-start.1 = ((bf16[8,32,1024]{2,1,0:T(8,128)(2,1)}), bf16[8,32,1024]{2,1,0:T(8,128)(2,1)S(1)}, u32[]{:S(2)}, u32[]{:S(2)}) async-start(bf16[8,32,1024]{2,1,0:T(8,128)(2,1)} %bitcast.10), calls=%async_computation.1 | async-start | bytes 1048576 | tf_op jit(solution)/shard_map/all_to_all | solution.py:652
  125.7 0.0 copy-done.5
  125.7 0.1 multiply_reduce_fusion
  125.8 14.3 %all-to-all-done.1 = bf16[8,32,1024]{2,1,0:T(8,128)(2,1)S(1)} async-done(((bf16[8,32,1024]{2,1,0:T(8,128)(2,1)}), bf16[8,32,1024]{2,1,0:T(8,128)(2,1)S(1)}, u32[]{:S(2)}, u32[]{:S(2)}) %all-to-all-start.1) | async-done | bytes 524320 | tf_op jit(solution)/shard_map/all_to_all | solution.py:652
  140.1 0.0 copy-done
  140.1 0.0 copy-done.2
  140.1 0.0 copy-done.3
  140.1 0.0 copy-done.4
  140.1 1.7 %traces.1 = f32[128,256]{1,0:T(8,128)} custom-call(s32[1,128]{1,0:T(1,128)S(1)} %bitcast.26, f32[1,128]{1,0:T(1,128)S(1)} %copy-done.3, f32[1,128]{1,0:T(1,128)S(1)} %copy-done.4, f32[1,128]{1,0:T(1,128)S(1)} %divide_bitcast_fusion.step, bf16[128,256]{1,0:T(8,128)(2,1)S(1)} %bitcast.24, bf16[256,1024]{1,0:T(8,128)(2,1)S(1)} %bitcast.22), custom_call_target="tpu_custom_call" | custom-call | flops 1 | bytes 1 | tf_op jit(solution)/shard_map/traces/pallas_call | solution.py:603
  (1 shorter events, 0.0 us)
Async XLA Ops:
  3.4 41.5 %all-to-all-start = ((bf16[8,32,2688]{2,1,0:T(8,128)(2,1)}), bf16[8,32,2688]{2,1,0:T(8,128)(2,1)S(1)}, u32[]{:S(2)}, u32[]{:S(2)}) async-start(bf16[8,32,2688]{2,1,0:T(8,128)(2,1)} %bitcast.27), calls=%async_computation | async-start | bytes 2752512 | tf_op jit(solution)/shard_map/all_to_all | solution.py:630
  13.7 97.7 %collective-permute-start = (bf16[8,256,256]{2,1,0:T(8,128)(2,1)}, bf16[8,256,256]{2,1,0:T(8,128)(2,1)S(1)}, u32[]{:S(2)}, u32[]{:S(2)}) collective-permute-start(bf16[8,256,256]{2,1,0:T(8,128)(2,1)} %get-tuple-element.39), channel_id=1, source_target_pairs={{0,4},{4,8},{8,12},{12,16},{16,20},{20,24},{24,28},{1,5},{5,9},{9,... | collective-permute-start | bytes 3145736 | tf_op jit(solution)/shard_map/ppermute | solution.py:633
  17.7 93.7 %collective-permute-start.1 = (bf16[8,256,256]{2,1,0:T(8,128)(2,1)}, bf16[8,256,256]{2,1,0:T(8,128)(2,1)S(1)}, u32[]{:S(2)}, u32[]{:S(2)}) collective-permute-start(bf16[8,256,256]{2,1,0:T(8,128)(2,1)} %get-tuple-element.38), channel_id=1, source_target_pairs={{4,0},{8,4},{12,8},{16,12},{20,16},{24,20},{28,24},{5,1},{9,5},{13... | collective-permute-start | bytes 3145736 | tf_op jit(solution)/shard_map/ppermute | solution.py:633
  21.3 41.2 %collective-permute-start.2 = (bf16[4,256,256]{2,1,0:T(8,128)(2,1)}, bf16[4,256,256]{2,1,0:T(8,128)(2,1)}, u32[]{:S(2)}, u32[]{:S(2)}) collective-permute-start(bf16[4,256,256]{2,1,0:T(8,128)(2,1)} %get-tuple-element.37), channel_id=1, source_target_pairs={{4,0},{8,4},{12,8},{16,12},{20,16},{24,20},{28,24},{5,1},{9,5},{13... | collective-permute-start | bytes 1572872 | tf_op jit(solution)/shard_map/ppermute | solution.py:633
  22.6 70.5 %collective-permute-start.3 = (bf16[4,256,256]{2,1,0:T(8,128)(2,1)}, bf16[4,256,256]{2,1,0:T(8,128)(2,1)}, u32[]{:S(2)}, u32[]{:S(2)}) collective-permute-start(bf16[4,256,256]{2,1,0:T(8,128)(2,1)} %get-tuple-element.36), channel_id=1, source_target_pairs={{0,4},{4,8},{8,12},{12,16},{16,20},{20,24},{24,28},{1,5},{5,9},{9,... | collective-permute-start | bytes 1572872 | tf_op jit(solution)/shard_map/ppermute | solution.py:633
  96.2 11.4 %copy-start.1 = (f32[1,256]{1,0:T(1,128)S(1)}, f32[1,256]{1,0:T(1,128)}, u32[]{:S(2)}) copy-start(f32[1,256]{1,0:T(1,128)} %gain.3) | copy-start | bytes 3076
  96.2 5.5 %collective-permute-start.4 = (f32[40,256]{1,0:T(8,128)S(1)}, f32[40,256]{1,0:T(8,128)S(1)}, u32[]{:S(2)}, u32[]{:S(2)}) collective-permute-start(f32[40,256]{1,0:T(8,128)S(1)} %get-tuple-element.25.noise), channel_id=1, source_target_pairs={{0,1},{1,2},{2,3},{4,5},{5,6},{6,7},{8,9},{9,10},{10,11},{12,13},{... | collective-permute-start | bytes 122888 | tf_op jit(solution)/shard_map/ppermute | solution.py:644
  97.5 4.8 %collective-permute-start.5 = (f32[40,256]{1,0:T(8,128)S(1)}, f32[40,256]{1,0:T(8,128)S(1)}, u32[]{:S(2)}, u32[]{:S(2)}) collective-permute-start(f32[40,256]{1,0:T(8,128)S(1)} %get-tuple-element.25.noise), channel_id=1, source_target_pairs={{1,0},{2,1},{3,2},{5,4},{6,5},{7,6},{9,8},{10,9},{11,10},{13,12},{... | collective-permute-start | bytes 122888 | tf_op jit(solution)/shard_map/ppermute | solution.py:645
  111.5 14.2 %copy-start.5 = (bf16[1,128,1024]{2,1,0:T(8,128)(2,1)S(1)}, bf16[1,128,1024]{2,1,0:T(8,128)(2,1)}, u32[]{:S(2)}) copy-start(bf16[1,128,1024]{2,1,0:T(8,128)(2,1)} %param.9) | copy-start | bytes 786436
  111.5 28.6 %copy-start = (bf16[1,128,256]{2,1,0:T(8,128)(2,1)S(1)}, bf16[1,128,256]{2,1,0:T(8,128)(2,1)}, u32[]{:S(2)}) copy-start(bf16[1,128,256]{2,1,0:T(8,128)(2,1)} %param.10) | copy-start | bytes 196612
  111.5 28.6 %copy-start.2 = (s32[1,128,1]{1,2,0:T(1,128)S(1)}, s32[1,128,1]{1,2,0:T(1,128)}, u32[]{:S(2)}) copy-start(s32[1,128,1]{1,2,0:T(1,128)} %param.11) | copy-start | bytes 1540
  111.5 28.6 %copy-start.3 = (f32[1,128]{1,0:T(1,128)S(1)}, f32[1,128]{1,0:T(1,128)}, u32[]{:S(2)}) copy-start(f32[1,128]{1,0:T(1,128)} %slow.1) | copy-start | bytes 1540
  111.5 28.6 %copy-start.4 = (f32[1,128]{1,0:T(1,128)S(1)}, f32[1,128]{1,0:T(1,128)}, u32[]{:S(2)}) copy-start(f32[1,128]{1,0:T(1,128)} %fast.1) | copy-start | bytes 1540
  116.2 23.9 %all-to-all-start.1 = ((bf16[8,32,1024]{2,1,0:T(8,128)(2,1)}), bf16[8,32,1024]{2,1,0:T(8,128)(2,1)S(1)}, u32[]{:S(2)}, u32[]{:S(2)}) async-start(bf16[8,32,1024]{2,1,0:T(8,128)(2,1)} %bitcast.10), calls=%async_computation.1 | async-start | bytes 1048576 | tf_op jit(solution)/shard_map/all_to_all | solution.py:652

commit v4 on v3

--- a/solution.py
+++ b/solution.py
@@ -633,9 +633,10 @@
         return (lax.ppermute(cut[0], "pix", pix_up), lax.ppermute(cut[1], "pix", pix_down))
 
     near_prev, near_next = exchange((frames_in[0, rows - NEAR :], frames_in[0, :NEAR]))
-    outer_prev, outer_next = exchange(
-        (frames_in[0, rows - RAD : rows - NEAR], frames_in[0, NEAR:RAD])
-    )
+    cut, inbox = lax.optimization_barrier(
+        ((frames_in[0, rows - RAD : rows - NEAR], frames_in[0, NEAR:RAD]), inbox)
+    )
+    outer_prev, outer_next = exchange(cut)
 
     foot_rows, residual, noise = make_residual(inbox, movie)
     near_rows, near_residual, noise = make_near(inbox, near_next, near_prev, noise)

time: 143 us -> 159 us (1.11)
  waiting for transfers between devices: 67.7 us -> 90.4 us
  starting transfers between devices: 32.1 us -> 27.2 us
    all_to_all x1, waiting for transfers between devices: 16.4 us -> 29.7 us  [on_device(): lax.all_to_all(outbox, 'pix', split_axis=0, concat_axis=0, tiled=True)]
    ppermute x2, waiting for transfers between devices: 5.77 us -> 16.3 us  [exchange(): lax.ppermute(cut[1], 'pix', pix_down)]
    all_to_all x1, starting transfers between devices: 9.51 us -> 5.95 us  [on_device(): lax.all_to_all(gradient, 'pix', split_axis=0, concat_axis=0, tiled=True)]
  transfers between devices with their start and end apart: 8 -> 8, of which waited for: 5 -> 5; matrix products, arithmetic and copies ran while one was open for 4% -> 3% of each run, Pallas kernels for 19% -> 16%
where the time goes in v4:
time: 159 us; the launch traced here: 158 us
  waiting for transfers between devices  90.4 us (57%)
  Pallas kernels  34.6 us (22%)
  starting transfers between devices  27.2 us (17%)
  local copies, waits for them, and re-layouts  4.37 us (3%)
    all_to_all x1, waiting for transfers between devices, on_device(): lax.all_to_all(outbox, 'pix', split_axis=0, concat_axis=0, tiled=True)  29.7 us
    ppermute x2, waiting for transfers between devices, exchange(): lax.ppermute(cut[0], 'pix', pix_up)  29.5 us
    ppermute x2, waiting for transfers between devices, exchange(): lax.ppermute(cut[1], 'pix', pix_down)  16.3 us
    all_to_all x1, waiting for transfers between devices, on_device(): lax.all_to_all(gradient, 'pix', split_axis=0, concat_axis=0, tiled=True)  14.3 us
    pallas_call x1, Pallas kernels, make_residual(): pl.pallas_call(residual_kernel, in_specs=[VMEM, HBM], out_specs=[HBM, HBM...  11.8 us
    ppermute x2, starting transfers between devices, exchange(): lax.ppermute(cut[0], 'pix', pix_up)  8.58 us
    pallas_call x2, Pallas kernels, call(): pl.pallas_call(kernel, in_specs=specs, out_specs=[HBM] + [VMEM] * (len(ou...  8.51 us
    all_to_all x1, starting transfers between devices, on_device(): lax.all_to_all(outbox, 'pix', split_axis=0, concat_axis=0, tiled=True)  7.29 us
  transfers between devices with their start and end apart: 8, of which 5 were waited for; matrix products, arithmetic and copies ran while one was open for 3% of the time, Pallas kernels for 16%

profile of v4, /device:TPU:0, one launch (start us, length us, event | category | flops | bytes accessed | tf_op | source)
XLA Modules:
  0.0 157.6 jit_solution(551714170624893805)
XLA Ops:
  0.6 2.7 %outbox.1 = bf16[256,2688]{1,0:T(8,128)(2,1)} custom-call(s32[1,128]{1,0:T(1,128)} %bitcast.25, s32[1,128]{1,0:T(1,128)} %refs_1_.1, bf16[128,1024]{1,0:T(8,128)(2,1)} %bitcast.28, bf16[128,256]{1,0:T(8,128)(2,1)} %bitcast.23), custom_call_target="tpu_custom_call" | custom-call | flops 1 | bytes 1 | tf_op jit(solution)/shard_map/outbox/pallas_call | solution.py:91
  3.4 7.3 %all-to-all-start = ((bf16[8,32,2688]{2,1,0:T(8,128)(2,1)}), bf16[8,32,2688]{2,1,0:T(8,128)(2,1)S(1)}, u32[]{:S(2)}, u32[]{:S(2)}) async-start(bf16[8,32,2688]{2,1,0:T(8,128)(2,1)} %bitcast.27), calls=%async_computation | async-start | bytes 2752512 | tf_op jit(solution)/shard_map/all_to_all | solution.py:630
  10.7 3.1 %slice_bitcast_fusion = (bf16[8,256,256]{2,1,0:T(8,128)(2,1)}, bf16[8,256,256]{2,1,0:T(8,128)(2,1)}) fusion(bf16[1,32,256,256]{3,2,1,0:T(8,128)(2,1)} %movie.1), kind=kLoop, calls=%fused_computation | loop fusion | bytes 4194304 | tf_op jit(solution)/shard_map/squeeze | solution.py:637
  13.7 29.7 %all-to-all-done = bf16[8,32,2688]{2,1,0:T(8,128)(2,1)S(1)} async-done(((bf16[8,32,2688]{2,1,0:T(8,128)(2,1)}), bf16[8,32,2688]{2,1,0:T(8,128)(2,1)S(1)}, u32[]{:S(2)}, u32[]{:S(2)}) %all-to-all-start) | async-done | bytes 1376288 | tf_op jit(solution)/shard_map/all_to_all | solution.py:630
  43.5 3.4 %collective-permute-start = (bf16[8,256,256]{2,1,0:T(8,128)(2,1)}, bf16[8,256,256]{2,1,0:T(8,128)(2,1)S(1)}, u32[]{:S(2)}, u32[]{:S(2)}) collective-permute-start(bf16[8,256,256]{2,1,0:T(8,128)(2,1)} %get-tuple-element.26), channel_id=1, source_target_pairs={{0,4},{4,8},{8,12},{12,16},{16,20},{20,24},{24,28},{1,5},{5,9},{9,... | collective-permute-start | bytes 3145736 | tf_op jit(solution)/shard_map/ppermute | solution.py:633
  46.8 1.3 collective-permute-start.1
  48.1 1.3 slice_bitcast_fusion.2
  49.4 1.3 collective-permute-start.2
  50.7 5.2 %collective-permute-start.3 = (bf16[4,256,256]{2,1,0:T(8,128)(2,1)S(1)}, bf16[4,256,256]{2,1,0:T(8,128)(2,1)S(1)}, u32[]{:S(2)}, u32[]{:S(2)}) collective-permute-start(bf16[4,256,256]{2,1,0:T(8,128)(2,1)S(1)} %get-tuple-element.42), channel_id=1, source_target_pairs={{0,4},{4,8},{8,12},{12,16},{16,20},{20,24},{24,28},{1,5},{5,9},{9,... | collective-permute-start | bytes 1572872 | tf_op jit(solution)/shard_map/ppermute | solution.py:633
  55.9 11.8 %residual.1 = (bf16[32,256,256]{2,1,0:T(8,128)(2,1)S(1)}, bf16[32,256,256]{2,1,0:T(8,128)(2,1)S(1)}, f32[8,4,256]{2,1,0:T(4,128)S(1)}) custom-call(bf16[256,2688]{1,0:T(8,128)(2,1)S(1)} %bitcast.19, bf16[1,32,256,256]{3,2,1,0:T(8,128)(2,1)} %movie.1), custom_call_target="tpu_custom_call" | custom-call | flops 1 | bytes 1 | tf_op jit(solution)/shard_map/residual/pallas_call | solution.py:212
  67.7 16.3 %collective-permute-done.2.movie_next = bf16[4,256,256]{2,1,0:T(8,128)(2,1)S(1)} collective-permute-done((bf16[4,256,256]{2,1,0:T(8,128)(2,1)S(1)}, bf16[4,256,256]{2,1,0:T(8,128)(2,1)S(1)}, u32[]{:S(2)}, u32[]{:S(2)}) %collective-permute-start.2) | collective-permute-done | bytes 524320 | tf_op jit(solution)/shard_map/ppermute | solution.py:633
  84.0 29.5 %collective-permute-done.3.movie_prev = bf16[4,256,256]{2,1,0:T(8,128)(2,1)S(1)} collective-permute-done((bf16[4,256,256]{2,1,0:T(8,128)(2,1)S(1)}, bf16[4,256,256]{2,1,0:T(8,128)(2,1)S(1)}, u32[]{:S(2)}, u32[]{:S(2)}) %collective-permute-start.3) | collective-permute-done | bytes 524320 | tf_op jit(solution)/shard_map/ppermute | solution.py:633
  113.6 1.9 %near.1 = (bf16[8,256,256]{2,1,0:T(8,128)(2,1)S(1)}, bf16[8,256,256]{2,1,0:T(8,128)(2,1)S(1)}, f32[40,256]{1,0:T(8,128)S(1)}) custom-call(bf16[256,2688]{1,0:T(8,128)(2,1)S(1)} %bitcast.20, bf16[4,256,256]{2,1,0:T(8,128)(2,1)S(1)} %collective-permute-done.2.movie_next, bf16[4,256,256]{2,1,0:T(8,128)(2,1)S(1)} %collective-permute-done.3.movie_prev, ...), custom_call_target="tpu_custom_call" | custom-call | flops 1 | bytes 1 | tf_op jit(solution)/shard_map/near/pallas_call | solution.py:257
  115.4 0.0 copy-start.1
  115.4 1.3 collective-permute-start.4
  116.7 1.5 collective-permute-start.5
  118.2 2.7 %outer_model.1.model = f32[16,256,256]{2,1,0:T(8,128)S(1)} custom-call(bf16[256,2688]{1,0:T(8,128)(2,1)S(1)} %bitcast.21), custom_call_target="tpu_custom_call" | custom-call | flops 1 | bytes 1 | tf_op jit(solution)/shard_map/outer_model/pallas_call | solution.py:282
  121.0 0.0 collective-permute-done.4.noise_before
  121.0 0.6 collective-permute-done.5.noise_after
  121.6 5.2 %weights.1 = (bf16[32,256,256]{2,1,0:T(8,128)(2,1)S(1)}, bf16[3,256,256]{2,1,0:T(8,128)(2,1)S(1)}, bf16[3,256,256]{2,1,0:T(8,128)(2,1)S(1)}) custom-call(bf16[32,256,256]{2,1,0:T(8,128)(2,1)S(1)} %get-tuple-element.28.own, bf16[8,256,256]{2,1,0:T(8,128)(2,1)S(1)} %get-tuple-element.30.near, f32[40,256]{1,0:T(8,128)S(1)} %get-tuple-element.31.noise, ...), custom_call_target="tpu_custom_call" | custom-call | flops 1 | bytes 1 | tf_op jit(solution)/shard_map/weights/pallas_call | solution.py:356
  126.8 0.0 copy-done.1
  126.8 3.9 %annulus_middle.1 = (bf16[1,32,256,256]{3,2,1,0:T(8,128)(2,1)}, f32[256,256]{1,0:T(8,128)S(1)}, f32[256,256]{1,0:T(8,128)S(1)}, f32[256,256]{1,0:T(8,128)S(1)}) custom-call(bf16[32,256,256]{2,1,0:T(8,128)(2,1)S(1)} %get-tuple-element.25.own, bf16[8,256,256]{2,1,0:T(8,128)(2,1)S(1)} %get-tuple-element.35.near, ...), custom_call_target="tpu_custom_call" | custom-call | flops 1 | bytes 1 | tf_op jit(solution)/shard_map/annulus_middle/pallas_call | solution.py:524
  130.7 0.0 collective-permute-done.movie_prev
  130.7 0.0 collective-permute-done.1.movie_next
  130.7 0.0 copy-start.5
  130.7 0.0 copy-start
  130.7 0.0 copy-start.2
  130.8 0.0 copy-start.3
  130.8 0.0 copy-start.4
  130.8 4.7 %annulus_ends.1 = (bf16[1,32,256,256]{3,2,1,0:T(8,128)(2,1)}, bf16[256,1024]{1,0:T(8,128)(2,1)}) custom-call(bf16[32,256,256]{2,1,0:T(8,128)(2,1)S(1)} %get-tuple-element.25.own, bf16[8,256,256]{2,1,0:T(8,128)(2,1)S(1)} %collective-permute-done.movie_prev, ...), custom_call_target="tpu_custom_call", output_to_operand_aliasing={{0}: (8, {})} | custom-call | flops 1 | bytes 1 | tf_op jit(solution)/shard_map/annulus_ends/pallas_call | solution.py:524
  135.4 6.0 %all-to-all-start.1 = ((bf16[8,32,1024]{2,1,0:T(8,128)(2,1)}), bf16[8,32,1024]{2,1,0:T(8,128)(2,1)S(1)}, u32[]{:S(2)}, u32[]{:S(2)}) async-start(bf16[8,32,1024]{2,1,0:T(8,128)(2,1)} %bitcast.10), calls=%async_computation.1 | async-start | bytes 1048576 | tf_op jit(solution)/shard_map/all_to_all | solution.py:653
  141.4 0.0 copy-done.5
  141.4 0.1 multiply_reduce_fusion
  141.5 14.3 %all-to-all-done.1 = bf16[8,32,1024]{2,1,0:T(8,128)(2,1)S(1)} async-done(((bf16[8,32,1024]{2,1,0:T(8,128)(2,1)}), bf16[8,32,1024]{2,1,0:T(8,128)(2,1)S(1)}, u32[]{:S(2)}, u32[]{:S(2)}) %all-to-all-start.1) | async-done | bytes 524320 | tf_op jit(solution)/shard_map/all_to_all | solution.py:653
  155.8 0.0 copy-done
  155.8 0.0 copy-done.2
  155.8 0.0 copy-done.3
  155.8 0.0 copy-done.4
  155.8 1.7 %traces.1 = f32[128,256]{1,0:T(8,128)} custom-call(s32[1,128]{1,0:T(1,128)S(1)} %bitcast.26, f32[1,128]{1,0:T(1,128)S(1)} %copy-done.3, f32[1,128]{1,0:T(1,128)S(1)} %copy-done.4, f32[1,128]{1,0:T(1,128)S(1)} %divide_bitcast_fusion.step, bf16[128,256]{1,0:T(8,128)(2,1)S(1)} %bitcast.24, bf16[256,1024]{1,0:T(8,128)(2,1)S(1)} %bitcast.22), custom_call_target="tpu_custom_call" | custom-call | flops 1 | bytes 1 | tf_op jit(solution)/shard_map/traces/pallas_call | solution.py:603
  (1 shorter events, 0.0 us)
Async XLA Ops:
  3.4 40.1 %all-to-all-start = ((bf16[8,32,2688]{2,1,0:T(8,128)(2,1)}), bf16[8,32,2688]{2,1,0:T(8,128)(2,1)S(1)}, u32[]{:S(2)}, u32[]{:S(2)}) async-start(bf16[8,32,2688]{2,1,0:T(8,128)(2,1)} %bitcast.27), calls=%async_computation | async-start | bytes 2752512 | tf_op jit(solution)/shard_map/all_to_all | solution.py:630
  43.5 87.2 %collective-permute-start = (bf16[8,256,256]{2,1,0:T(8,128)(2,1)}, bf16[8,256,256]{2,1,0:T(8,128)(2,1)S(1)}, u32[]{:S(2)}, u32[]{:S(2)}) collective-permute-start(bf16[8,256,256]{2,1,0:T(8,128)(2,1)} %get-tuple-element.26), channel_id=1, source_target_pairs={{0,4},{4,8},{8,12},{12,16},{16,20},{20,24},{24,28},{1,5},{5,9},{9,... | collective-permute-start | bytes 3145736 | tf_op jit(solution)/shard_map/ppermute | solution.py:633
  46.8 83.9 %collective-permute-start.1 = (bf16[8,256,256]{2,1,0:T(8,128)(2,1)}, bf16[8,256,256]{2,1,0:T(8,128)(2,1)S(1)}, u32[]{:S(2)}, u32[]{:S(2)}) collective-permute-start(bf16[8,256,256]{2,1,0:T(8,128)(2,1)} %get-tuple-element.27), channel_id=1, source_target_pairs={{4,0},{8,4},{12,8},{16,12},{20,16},{24,20},{28,24},{5,1},{9,5},{13... | collective-permute-start | bytes 3145736 | tf_op jit(solution)/shard_map/ppermute | solution.py:633
  49.4 34.6 %collective-permute-start.2 = (bf16[4,256,256]{2,1,0:T(8,128)(2,1)S(1)}, bf16[4,256,256]{2,1,0:T(8,128)(2,1)S(1)}, u32[]{:S(2)}, u32[]{:S(2)}) collective-permute-start(bf16[4,256,256]{2,1,0:T(8,128)(2,1)S(1)} %get-tuple-element.43), channel_id=1, source_target_pairs={{4,0},{8,4},{12,8},{16,12},{20,16},{24,20},{28,24},{5,1},{9,5},{13... | collective-permute-start | bytes 1572872 | tf_op jit(solution)/shard_map/ppermute | solution.py:633
  50.7 62.8 %collective-permute-start.3 = (bf16[4,256,256]{2,1,0:T(8,128)(2,1)S(1)}, bf16[4,256,256]{2,1,0:T(8,128)(2,1)S(1)}, u32[]{:S(2)}, u32[]{:S(2)}) collective-permute-start(bf16[4,256,256]{2,1,0:T(8,128)(2,1)S(1)} %get-tuple-element.42), channel_id=1, source_target_pairs={{0,4},{4,8},{8,12},{12,16},{16,20},{20,24},{24,28},{1,5},{5,9},{9,... | collective-permute-start | bytes 1572872 | tf_op jit(solution)/shard_map/ppermute | solution.py:633
  115.4 11.4 %copy-start.1 = (f32[1,256]{1,0:T(1,128)S(1)}, f32[1,256]{1,0:T(1,128)}, u32[]{:S(2)}) copy-start(f32[1,256]{1,0:T(1,128)} %gain.3) | copy-start | bytes 3076
  115.4 5.5 %collective-permute-start.4 = (f32[40,256]{1,0:T(8,128)S(1)}, f32[40,256]{1,0:T(8,128)S(1)}, u32[]{:S(2)}, u32[]{:S(2)}) collective-permute-start(f32[40,256]{1,0:T(8,128)S(1)} %get-tuple-element.31.noise), channel_id=1, source_target_pairs={{0,1},{1,2},{2,3},{4,5},{5,6},{6,7},{8,9},{9,10},{10,11},{12,13},{... | collective-permute-start | bytes 122888 | tf_op jit(solution)/shard_map/ppermute | solution.py:645
  116.7 4.8 %collective-permute-start.5 = (f32[40,256]{1,0:T(8,128)S(1)}, f32[40,256]{1,0:T(8,128)S(1)}, u32[]{:S(2)}, u32[]{:S(2)}) collective-permute-start(f32[40,256]{1,0:T(8,128)S(1)} %get-tuple-element.31.noise), channel_id=1, source_target_pairs={{1,0},{2,1},{3,2},{5,4},{6,5},{7,6},{9,8},{10,9},{11,10},{13,12},{... | collective-permute-start | bytes 122888 | tf_op jit(solution)/shard_map/ppermute | solution.py:646
  130.7 10.7 %copy-start.5 = (bf16[1,128,1024]{2,1,0:T(8,128)(2,1)S(1)}, bf16[1,128,1024]{2,1,0:T(8,128)(2,1)}, u32[]{:S(2)}) copy-start(bf16[1,128,1024]{2,1,0:T(8,128)(2,1)} %param.9) | copy-start | bytes 786436
  130.7 25.1 %copy-start = (bf16[1,128,256]{2,1,0:T(8,128)(2,1)S(1)}, bf16[1,128,256]{2,1,0:T(8,128)(2,1)}, u32[]{:S(2)}) copy-start(bf16[1,128,256]{2,1,0:T(8,128)(2,1)} %param.10) | copy-start | bytes 196612
  130.7 25.1 %copy-start.2 = (s32[1,128,1]{1,2,0:T(1,128)S(1)}, s32[1,128,1]{1,2,0:T(1,128)}, u32[]{:S(2)}) copy-start(s32[1,128,1]{1,2,0:T(1,128)} %param.11) | copy-start | bytes 1540
  130.8 25.1 %copy-start.3 = (f32[1,128]{1,0:T(1,128)S(1)}, f32[1,128]{1,0:T(1,128)}, u32[]{:S(2)}) copy-start(f32[1,128]{1,0:T(1,128)} %slow.1) | copy-start | bytes 1540
  130.8 25.0 %copy-start.4 = (f32[1,128]{1,0:T(1,128)S(1)}, f32[1,128]{1,0:T(1,128)}, u32[]{:S(2)}) copy-start(f32[1,128]{1,0:T(1,128)} %fast.1) | copy-start | bytes 1540
  135.4 20.4 %all-to-all-start.1 = ((bf16[8,32,1024]{2,1,0:T(8,128)(2,1)}), bf16[8,32,1024]{2,1,0:T(8,128)(2,1)S(1)}, u32[]{:S(2)}, u32[]{:S(2)}) async-start(bf16[8,32,1024]{2,1,0:T(8,128)(2,1)} %bitcast.10), calls=%async_computation.1 | async-start | bytes 1048576 | tf_op jit(solution)/shard_map/all_to_all | solution.py:653
